TPU v7x, 32 devices: a whole 2x2x4 slice. The times are simulated.
32 devices in a mesh: aux: 8 (over z, y), occ: 4 (over x, core).
Axes of the slice: x: 2, y: 2, z: 4, core: 2. Of those that a mesh axis runs over, the one named last changes fastest.
Arguments:
- factors: bfloat16 [256, 128, 384], P('occ', 'aux'), may hold values from -1 to 1
- response: bfloat16 [256, 128, 384], P('occ', 'aux'), may hold values from -1 to 1
- pattern: int32 [3, 3], replicated, may hold values 0 or 1
Outputs:
- exchange_k: float32 [384, 384], P('aux', 'occ')
All inputs are finite; a program needn't handle non-finite values.
Results may differ from a plain program's by a relative error of at most 0.0003.
Values sent between devices are 32-bit elements; how exact they have to be, the bound alone decides.
No kernel may reach another device: no remote copies, remote signals or barrier semaphores. Data moves between devices by JAX's collectives and lax.ppermute only.
A program may use at most 64 MiB of HBM per device.

v0:
```python
import jax
import jax.numpy as jnp
from jax import lax
from jax.sharding import PartitionSpec as P


def shards(factors, response, pattern):
    nocc_dev, aux_dev, nbasis = factors.shape
    ground_rows = factors.reshape(nocc_dev * aux_dev, nbasis)
    response_rows = response.reshape(nocc_dev * aux_dev, nbasis)
    nblocks = pattern.shape[0]
    blk_width = nbasis // nblocks
    tile_table = pattern.astype(jnp.float32)
    own_cols = nbasis // lax.axis_size("occ")
    occ_index = lax.axis_index("occ")
    row_share = nbasis // lax.axis_size("aux")
    cross = lax.dot_general(
        ground_rows, response_rows, (((0,), (0,)), ((), ())), preferred_element_type=jnp.float32
    )
    block_ids = jnp.arange(row_share * lax.axis_size("aux"), dtype=jnp.int32) // blk_width
    onehot = (block_ids[:, None] == jnp.arange(nblocks, dtype=jnp.int32)[None, :]).astype(
        jnp.float32
    )
    picked = jnp.dot(onehot, tile_table, precision=lax.Precision.HIGHEST)
    own_rows = lax.psum_scatter(
        jnp.repeat(picked, blk_width, axis=1) * cross, "aux", scatter_dimension=0, tiled=True
    )
    turned = lax.all_to_all(own_rows, "aux", split_axis=1, concat_axis=0, tiled=True)
    own_rows = 0.5 * (own_rows + turned.T)
    summed = lax.psum(own_rows, "occ")
    result = lax.dynamic_slice_in_dim(summed, occ_index * own_cols, own_cols, 1)
    return result


def solution(mesh):
    in_specs = (P("occ", "aux", None), P("occ", "aux", None), P())
    out_specs = P("aux", "occ")
    return jax.shard_map(shards, mesh=mesh, in_specs=in_specs, out_specs=out_specs, check_vma=False)
```

profile of v0, /device:TPU:1, one launch (start us, length us, event | category | flops | bytes accessed | tf_op | source)
XLA Modules:
  0.0 125.4 jit_solution(13153715279281606696)
XLA Ops:
  6.5 0.0 copy-start
  6.5 0.0 reduce-scatter.2.cloned.1.call-start
  6.5 1.1 fusion.1
  7.6 0.0 copy-start.2
  7.6 0.1 broadcast_in_dim.2
  7.7 0.2 copy.12
  7.9 0.0 copy-done
  7.9 0.9 copy-done.2
  8.8 1.4 %fusion = f32[384,384]{1,0:T(8,128)} fusion(f32[384,384]{1,0:T(8,128)S(1)} %copy.12, bf16[64,16,384]{2,1,0:T(8,128)(2,1)S(1)} %copy-done, bf16[64,16,384]{2,1,0:T(8,128)(2,1)S(1)} %copy-done.2), kind=kOutput, calls=%fused_computation.1 | convolution fusion | flops 302137344 | bytes 2752512 | tf_op jit(solution)/shard_map/dot_general | solution.py:17
  10.2 0.0 reduce-scatter.2.cloned.1.call-update
  10.2 0.0 all-reduce.2.cloned.1.call-start
  10.2 62.8 %reduce-scatter.2.cloned.1.call-done = f32[48,384]{1,0:T(8,128)} async-done(((f32[384,384]{1,0:T(8,128)}), f32[48,384]{1,0:T(8,128)}) %reduce-scatter.2.cloned.1.call-update) | async-done | bytes 73744 | tf_op jit(solution)/shard_map/reduce_scatter | solution.py:25
  73.0 1.0 copy.15
  74.1 0.2 reshape.23
  74.3 9.0 %all_to_all.19 = f32[8,1,2304]{2,1,0:T(1,128)S(1)} all-to-all(f32[8,1,2304]{2,1,0:T(1,128)S(1)} %reshape.23), channel_id=1, replica_groups=mesh['aux'=8,'occ'=4] {'aux'}, dimensions={0} | all-to-all | bytes 147456 | tf_op jit(solution)/shard_map/all_to_all | solution.py:28
  83.3 0.5 broadcast.29
  83.8 0.8 reduce
  84.6 0.1 reshape.24
  84.8 0.1 copy.14
  84.9 0.0 copy-start.1
  84.9 0.1 all_to_all.17
  85.0 0.8 copy-done.1
  85.8 0.6 fusion.3
  86.4 0.0 all-reduce.2.cloned.1.call-update
  86.4 30.7 %all-reduce.2.cloned.1.call-done = f32[48,384]{1,0:T(8,128)} async-done(((f32[48,384]{1,0:T(8,128)}), f32[48,384]{1,0:T(8,128)}) %all-reduce.2.cloned.1.call-update) | async-done | bytes 73744 | tf_op jit(solution)/shard_map/psum | solution.py:30
  117.1 1.5 %constant_dynamic-slice_fusion = f32[48,96]{1,0:T(8,128)} fusion(f32[48,384]{1,0:T(8,128)} %all-reduce.2.cloned.1.call-done, s32[]{:T(128)S(6)} %select_n.13), kind=kLoop, calls=%fused_computation.15 | loop fusion | bytes 36868 | tf_op jit(solution)/shard_map/dynamic_slice | solution.py:31
  (2 shorter events, 0.0 us)
Async XLA Ops:
  6.5 1.4 %copy-start = (bf16[64,16,384]{2,1,0:T(8,128)(2,1)S(1)}, bf16[64,16,384]{2,1,0:T(8,128)(2,1)}, u32[]{:S(2)}) copy-start(bf16[64,16,384]{2,1,0:T(8,128)(2,1)} %param.3) | copy-start | bytes 2359300
  6.5 66.5 %reduce-scatter.2.cloned.1.call-start = ((), (), s32[]{:S(2)}) async-start(), calls=%async_computation.2 | async-start | bytes 663552 | tf_op jit(solution)/shard_map/reduce_scatter | solution.py:25
  7.6 1.2 copy-start.2
  10.2 106.9 %all-reduce.2.cloned.1.call-start = ((), (), s32[]{:S(2)}) async-start(), calls=%async_computation.3 | async-start | bytes 147456 | tf_op jit(solution)/shard_map/psum | solution.py:30
  84.9 0.9 copy-start.1
Sparse Core Ops, SparseCore 0:
  10.6 62.3 reduce-scatter.1
  86.5 30.5 all-reduce.1
where the time goes:
time: 126 us; the launch traced here: 125 us
  waiting for transfers between devices  93.5 us (74%)
  between operations  13.5 us (11%)
  blocking collectives  9.05 us (7%)
  local copies, waits for them, and re-layouts  5.43 us (4%)
  matrix products  2.46 us (2%)
  other arithmetic  1.46 us (1%)
    reduce_scatter x1, waiting for transfers between devices, shards(): lax.psum_scatter(jnp.repeat(picked, blk_width, axis=1) * cross, 'aux', sc...  62.8 us
    psum x1, waiting for transfers between devices, shards(): summed = lax.psum(own_rows, 'occ')  30.7 us
    all_to_all x1, blocking collectives, shards(): lax.all_to_all(own_rows, 'aux', split_axis=1, concat_axis=0, tiled=True)  9.05 us
  transfers between devices with their start and end apart: 2, of which 2 were waited for; matrix products, arithmetic and copies ran while one was open for 0% of the time, Pallas kernels for 0%

commit v1 on v0

v1 whole, which is shorter than its diff:
```python
import functools

import jax
import jax.numpy as jnp
from jax import lax
from jax.experimental import pallas as pl
from jax.experimental.pallas import tpu as pltpu
from jax.sharding import PartitionSpec as P

BOTH = ("aux", "occ")
CORE, X, Y, Z1, Z2 = 1, 2, 4, 8, 16
PLANE = (X | Y | CORE, X, Y | CORE)
LINE = (Z1 | Z2 | CORE, Z2 | CORE, Z1)
CHUNKS = 4


def swap(value, mask):
    return lax.ppermute(value, BOTH, [(i, i ^ mask) for i in range(32)])


def pack_kernel(pattern_hbm, ground_hbm, response_hbm, away_ref, stay_ref, ground, response, pattern, product, tiles, sems):
    depth, nbasis = ground.shape
    step = depth // CHUNKS
    nblocks = pattern.shape[0]
    blk = nbasis // nblocks
    rows, cols = nbasis // 8, nbasis // 4
    part = cols // 3

    copies = []
    for k in range(CHUNKS):
        here = pl.ds(k * step, step)
        copies.append(pltpu.make_async_copy(ground_hbm.at[here], ground.at[here], sems.at[2 * k]))
        copies.append(pltpu.make_async_copy(response_hbm.at[here], response.at[here], sems.at[2 * k + 1]))
    masks = pltpu.make_async_copy(pattern_hbm, pattern, sems.at[2 * CHUNKS])
    for copy in copies:
        copy.start()
    masks.start()
    for k in range(CHUNKS):
        copies[2 * k].wait()
        copies[2 * k + 1].wait()
        here = pl.ds(k * step, step)
        term = lax.dot_general(
            ground[here, :], response[here, :], (((0,), (0,)), ((), ())), preferred_element_type=jnp.float32
        )
        if k == 0:
            product[...] = term
        else:
            product[...] += term
    masks.wait()

    for i in range(nblocks):
        for j in range(i, nblocks):
            upper = 0.5 * pattern[i, j].astype(jnp.float32)
            lower = 0.5 * pattern[j, i].astype(jnp.float32)
            at_i, at_j = slice(i * blk, (i + 1) * blk), slice(j * blk, (j + 1) * blk)
            both = upper * product[at_i, at_j] + lower * product[at_j, at_i].T
            product[at_i, at_j] = both
            if i != j:
                product[at_j, at_i] = both.T
    for o in range(4):
        tiles[o, :, 0:cols] = product[:, o * cols : (o + 1) * cols]

    aux, occ = lax.axis_index("aux"), lax.axis_index("occ")
    z, y, x, core = aux // 2, aux % 2, occ // 2, occ % 2
    kind = core ^ y ^ (z // 2)
    lane = lax.broadcasted_iota(jnp.int32, (rows, 128), 1)
    for out_ref, flip in ((away_ref, 1), (stay_ref, 0)):
        for group in range(4):
            x_to, y_to = x ^ (group % 2), y ^ (group // 2)
            picked = []
            for turn in range(4):
                z_to = z ^ turn
                core_to = kind ^ flip ^ y_to ^ (z_to // 2)
                picked.append(tiles[2 * x_to + core_to, pl.ds(rows * (2 * z_to + y_to), rows), :])
            for turn in (1, 2, 3):
                own = pltpu.roll(picked[0], cols - part * (turn - 1), 1)
                at = group * 3 * rows + (turn - 1) * rows
                out_ref[pl.ds(at, rows), :] = jnp.where(lane < cols, picked[turn], own)


def fast_shards(factors, response, pattern):
    nocc_dev, aux_dev, nbasis = factors.shape
    depth = nocc_dev * aux_dev
    rows, cols = nbasis // 8, nbasis // 4
    part = cols // 3
    half = jax.ShapeDtypeStruct((12 * rows, 128), jnp.float32)
    away, stay = pl.pallas_call(
        pack_kernel,
        out_shape=(half, half),
        in_specs=[pl.BlockSpec(memory_space=pl.ANY)] * 3,
        out_specs=(pl.BlockSpec(memory_space=pltpu.VMEM),) * 2,
        scratch_shapes=[
            pltpu.VMEM((depth, nbasis), jnp.bfloat16),
            pltpu.VMEM((depth, nbasis), jnp.bfloat16),
            pltpu.SMEM(pattern.shape, jnp.int32),
            pltpu.VMEM((nbasis, nbasis), jnp.float32),
            pltpu.VMEM((4, nbasis, 128), jnp.float32),
            pltpu.SemaphoreType.DMA((2 * CHUNKS + 1,)),
        ],
        compiler_params=pltpu.CompilerParams(vmem_limit_bytes=32 * 1024 * 1024),
    )(pattern, factors.reshape(depth, nbasis), response.reshape(depth, nbasis))
    chip = (stay + swap(away, CORE)).reshape(4, 3 * rows, 128)
    order = {X: 1, Y | CORE: 2, X | Y | CORE: 3}
    plane = [swap(chip[order[mask]], mask) for mask in PLANE]
    line = (chip[0] + plane[0] + plane[1] + plane[2]).reshape(3, rows, 128)
    turns = {Z1: 0, Z2 | CORE: 1, Z1 | Z2 | CORE: 2}
    last = [swap(line[turns[mask]], mask) for mask in LINE]
    own = jnp.concatenate([line[0, :, cols:], line[1, :, cols:], line[2, :, cols:]], axis=1)
    return own + last[0][:, :cols] + last[1][:, :cols] + last[2][:, :cols]


def any_shards(factors, response, pattern):
    nocc_dev, aux_dev, nbasis = factors.shape
    ground_rows = factors.reshape(nocc_dev * aux_dev, nbasis)
    response_rows = response.reshape(nocc_dev * aux_dev, nbasis)
    blk = nbasis // pattern.shape[0]
    own_cols = nbasis // lax.axis_size("occ")
    cross = lax.dot_general(
        ground_rows, response_rows, (((0,), (0,)), ((), ())), preferred_element_type=jnp.float32
    )
    masked = jnp.repeat(jnp.repeat(pattern.astype(jnp.float32), blk, axis=0), blk, axis=1) * cross
    both = 0.5 * (masked + masked.T)
    own_rows = lax.psum_scatter(both, "aux", scatter_dimension=0, tiled=True)
    summed = lax.psum(own_rows, "occ")
    return lax.dynamic_slice_in_dim(summed, lax.axis_index("occ") * own_cols, own_cols, 1)


def solution(mesh):
    in_specs = (P("occ", "aux", None), P("occ", "aux", None), P())
    out_specs = P("aux", "occ")
    sizes = dict(mesh.shape)
    shards = fast_shards if sizes["aux"] == 8 and sizes["occ"] == 4 else any_shards
    return jax.shard_map(shards, mesh=mesh, in_specs=in_specs, out_specs=out_specs, check_vma=False)
```

time: 126 us -> 25.4 us (0.20)
  waiting for transfers between devices: 93.5 us -> 8.92 us
  between operations: 13.5 us -> 0.04 us
  blocking collectives: 9.05 us -> 0 us
  starting transfers between devices: 0.04 us -> 8.75 us
  Pallas kernels: 0 us -> 3.71 us
  matrix products: 2.46 us -> 0 us
  local copies, waits for them, and re-layouts: 5.43 us -> 3.05 us
    reduce_scatter x1 -> x0, waiting for transfers between devices: 62.8 us -> none  [shards(): lax.psum_scatter(jnp.repeat(picked, blk_width, axis=1) * cross, 'aux', sc...]
    psum x1 -> x0, waiting for transfers between devices: 30.7 us -> none  [shards(): summed = lax.psum(own_rows, 'occ')]
    all_to_all x1 -> x0, blocking collectives: 9.05 us -> none  [shards(): lax.all_to_all(own_rows, 'aux', split_axis=1, concat_axis=0, tiled=True)]
    ppermute x0 -> x7, waiting for transfers between devices: none -> 8.92 us  [swap(): return lax.ppermute(value, BOTH, [(i, i ^ mask) for i in range(32)])]
    ppermute x0 -> x7, starting transfers between devices: none -> 8.75 us  [swap(): return lax.ppermute(value, BOTH, [(i, i ^ mask) for i in range(32)])]
    pallas_call x0 -> x1, Pallas kernels: none -> 3.71 us  [fast_shards(): pl.pallas_call(pack_kernel, out_shape=(half, half), in_specs=[pl.BlockSpe...]
    dot_general x2 -> x0, matrix products: 2.46 us -> none  [the longest x1 1.41 us: shards(): lax.dot_general(ground_rows, response_rows, (((0,), (0,)), ((), ())), pre...]
    all_to_all x5 -> x0, local copies, waits for them, and re-layouts: 1.71 us -> none  [shards(): lax.all_to_all(own_rows, 'aux', split_axis=1, concat_axis=0, tiled=True)]
  transfers between devices with their start and end apart: 2 -> 7, of which waited for: 2 -> 6; matrix products, arithmetic and copies ran while one was open for 0% -> 0% of each run, Pallas kernels for 0% -> 0%
where the time goes in v1:
time: 25.4 us; the launch traced here: 25.2 us
  waiting for transfers between devices  8.92 us (35%)
  starting transfers between devices  8.75 us (34%)
  Pallas kernels  3.71 us (15%)
  local copies, waits for them, and re-layouts  3.05 us (12%)
  other arithmetic  0.75 us (3%)
    ppermute x7, waiting for transfers between devices, swap(): return lax.ppermute(value, BOTH, [(i, i ^ mask) for i in range(32)])  8.92 us
    ppermute x7, starting transfers between devices, swap(): return lax.ppermute(value, BOTH, [(i, i ^ mask) for i in range(32)])  8.75 us
    pallas_call x1, Pallas kernels, fast_shards(): pl.pallas_call(pack_kernel, out_shape=(half, half), in_specs=[pl.BlockSpe...  3.71 us
    unnamed x6, local copies, waits for them, and re-layouts  2.95 us
    add x1, other arithmetic, fast_shards(): return own + last[0][:, :cols] + last[1][:, :cols] + last[2][:, :cols]  0.7 us
  transfers between devices with their start and end apart: 7, of which 6 were waited for; matrix products, arithmetic and copies ran while one was open for 0% of the time, Pallas kernels for 0%

profile of v1, /device:TPU:1, one launch (start us, length us, event | category | flops | bytes accessed | tf_op | source)
XLA Modules:
  0.0 25.2 jit_solution(17533117626931639864)
XLA Ops:
  0.0 0.0 copy-start.2
  0.0 0.7 %copy-done.2 = s32[3,3]{1,0:T(4,128)S(1)} copy-done((s32[3,3]{1,0:T(4,128)S(1)}, s32[3,3]{1,0:T(4,128)}, u32[]{:S(2)}) %copy-start.2) | copy-done | bytes 60
  0.7 0.0 copy-start
  0.7 1.1 %copy-done = bf16[64,16,384]{2,1,0:T(8,128)(2,1)S(1)} copy-done((bf16[64,16,384]{2,1,0:T(8,128)(2,1)S(1)}, bf16[64,16,384]{2,1,0:T(8,128)(2,1)}, u32[]{:S(2)}) %copy-start) | copy-done | bytes 786456
  1.8 0.0 copy-start.1
  1.8 1.1 %copy-done.1 = bf16[64,16,384]{2,1,0:T(8,128)(2,1)S(1)} copy-done((bf16[64,16,384]{2,1,0:T(8,128)(2,1)S(1)}, bf16[64,16,384]{2,1,0:T(8,128)(2,1)}, u32[]{:S(2)}) %copy-start.1) | copy-done | bytes 786456
  3.0 3.7 %shard_map.37 = (f32[576,128]{1,0:T(8,128)S(1)}, f32[576,128]{1,0:T(8,128)S(1)}) custom-call(s32[3,3]{1,0:T(4,128)S(1)} %copy-done.2, bf16[1024,384]{1,0:T(8,128)(2,1)S(1)} %bitcast.9, bf16[1024,384]{1,0:T(8,128)(2,1)S(1)} %bitcast.10), custom_call_target="tpu_custom_call" | custom-call | tf_op jit(solution)/shard_map/pallas_call | solution.py:87
  6.7 0.1 collective-permute-start
  6.8 1.5 %collective-permute-done = f32[576,128]{1,0:T(8,128)S(1)} collective-permute-done((f32[576,128]{1,0:T(8,128)S(1)}, f32[576,128]{1,0:T(8,128)S(1)}, u32[]{:S(2)}, u32[]{:S(2)}) %collective-permute-start) | collective-permute-done | bytes 294944 | tf_op jit(solution)/shard_map/ppermute | solution.py:18
  8.4 3.6 %collective-permute-start.1 = (f32[144,128]{1,0:T(8,128)S(1)}, f32[144,128]{1,0:T(8,128)S(1)}, u32[]{:S(2)}, u32[]{:S(2)}) collective-permute-start(f32[144,128]{1,0:T(8,128)S(1)} %get-tuple-element.9), channel_id=1, source_target_pairs={{0,7},{1,6},{2,5},{3,4},{4,3},{5,2},{6,1},{7,0},{8,15},{9,14},{10,... | collective-permute-start | bytes 221192 | tf_op jit(solution)/shard_map/ppermute | solution.py:18
  12.0 0.3 %collective-permute-start.3 = (f32[144,128]{1,0:T(8,128)S(1)}, f32[144,128]{1,0:T(8,128)S(1)}, u32[]{:S(2)}, u32[]{:S(2)}) collective-permute-start(f32[144,128]{1,0:T(8,128)S(1)} %get-tuple-element.10), channel_id=1, source_target_pairs={{0,5},{1,4},{2,7},{3,6},{4,1},{5,0},{6,3},{7,2},{8,13},{9,12},{10,... | collective-permute-start | bytes 221192 | tf_op jit(solution)/shard_map/ppermute | solution.py:18
  12.3 0.1 collective-permute-start.2
  12.4 1.9 %collective-permute-done.1 = f32[144,128]{1,0:T(8,128)S(1)} collective-permute-done((f32[144,128]{1,0:T(8,128)S(1)}, f32[144,128]{1,0:T(8,128)S(1)}, u32[]{:S(2)}, u32[]{:S(2)}) %collective-permute-start.1) | collective-permute-done | bytes 73760 | tf_op jit(solution)/shard_map/ppermute | solution.py:18
  14.3 2.0 %collective-permute-done.3 = f32[144,128]{1,0:T(8,128)S(1)} collective-permute-done((f32[144,128]{1,0:T(8,128)S(1)}, f32[144,128]{1,0:T(8,128)S(1)}, u32[]{:S(2)}, u32[]{:S(2)}) %collective-permute-start.3) | collective-permute-done | bytes 73760 | tf_op jit(solution)/shard_map/ppermute | solution.py:18
  16.3 0.0 collective-permute-done.2
  16.4 4.0 %collective-permute-start.4 = (f32[48,128]{1,0:T(8,128)S(1)}, f32[48,128]{1,0:T(8,128)S(1)}, u32[]{:S(2)}, u32[]{:S(2)}) collective-permute-start(f32[48,128]{1,0:T(8,128)S(1)} %get-tuple-element.15), channel_id=1, source_target_pairs={{0,25},{1,24},{2,27},{3,26},{4,29},{5,28},{6,31},{7,30},{8,17},{9,... | collective-permute-start | bytes 73736 | tf_op jit(solution)/shard_map/ppermute | solution.py:18
  20.4 0.0 collective-permute-start.6
  20.4 0.6 %collective-permute-start.5 = (f32[48,128]{1,0:T(8,128)S(1)}, f32[48,128]{1,0:T(8,128)S(1)}, u32[]{:S(2)}, u32[]{:S(2)}) collective-permute-start(f32[48,128]{1,0:T(8,128)S(1)} %get-tuple-element.17), channel_id=1, source_target_pairs={{0,17},{1,16},{2,19},{3,18},{4,21},{5,20},{6,23},{7,22},{8,25},{9,... | collective-permute-start | bytes 73736 | tf_op jit(solution)/shard_map/ppermute | solution.py:18
  21.0 0.1 slice_bitcast_fusion.2
  21.1 1.0 %collective-permute-done.4 = f32[48,128]{1,0:T(8,128)S(1)} collective-permute-done((f32[48,128]{1,0:T(8,128)S(1)}, f32[48,128]{1,0:T(8,128)S(1)}, u32[]{:S(2)}, u32[]{:S(2)}) %collective-permute-start.4) | collective-permute-done | bytes 24608 | tf_op jit(solution)/shard_map/ppermute | solution.py:18
  22.1 0.9 %collective-permute-done.6 = f32[48,128]{1,0:T(8,128)S(1)} collective-permute-done((f32[48,128]{1,0:T(8,128)S(1)}, f32[48,128]{1,0:T(8,128)S(1)}, u32[]{:S(2)}, u32[]{:S(2)}) %collective-permute-start.6) | collective-permute-done | bytes 24608 | tf_op jit(solution)/shard_map/ppermute | solution.py:18
  23.0 1.5 %collective-permute-done.5 = f32[48,128]{1,0:T(8,128)S(1)} collective-permute-done((f32[48,128]{1,0:T(8,128)S(1)}, f32[48,128]{1,0:T(8,128)S(1)}, u32[]{:S(2)}, u32[]{:S(2)}) %collective-permute-start.5) | collective-permute-done | bytes 24608 | tf_op jit(solution)/shard_map/ppermute | solution.py:18
  24.5 0.7 %slice_add_fusion.1 = f32[48,96]{1,0:T(8,128)} fusion(f32[48,128]{1,0:T(8,128)S(1)} %collective-permute-done.6, f32[48,128]{1,0:T(8,128)S(1)} %collective-permute-done.5, f32[48,128]{1,0:T(8,128)S(1)} %collective-permute-done.4, f32[48,32]{1,0:T(8,128)S(1)} %get-tuple-element.13, f32[48,32]{1,0:T(8,128)S(1)} %get-tuple-element.14, ...), kind=kLoop, calls=%fused_computation.3 | loop fusion | flops 23040 | bytes 92160 | tf_op jit(solution)/shard_map/add | solution.py:109
  (4 shorter events, 0.1 us)
Async XLA Ops:
  0.0 0.7 %copy-start.2 = (s32[3,3]{1,0:T(4,128)S(1)}, s32[3,3]{1,0:T(4,128)}, u32[]{:S(2)}) copy-start(s32[3,3]{1,0:T(4,128)} %pattern_hbm.1) | copy-start | bytes 112
  0.7 1.1 %copy-start = (bf16[64,16,384]{2,1,0:T(8,128)(2,1)S(1)}, bf16[64,16,384]{2,1,0:T(8,128)(2,1)}, u32[]{:S(2)}) copy-start(bf16[64,16,384]{2,1,0:T(8,128)(2,1)} %param.3) | copy-start | bytes 2359300
  1.8 1.1 %copy-start.1 = (bf16[64,16,384]{2,1,0:T(8,128)(2,1)S(1)}, bf16[64,16,384]{2,1,0:T(8,128)(2,1)}, u32[]{:S(2)}) copy-start(bf16[64,16,384]{2,1,0:T(8,128)(2,1)} %param.4) | copy-start | bytes 2359300
  6.7 1.6 %collective-permute-start = (f32[576,128]{1,0:T(8,128)S(1)}, f32[576,128]{1,0:T(8,128)S(1)}, u32[]{:S(2)}, u32[]{:S(2)}) collective-permute-start(f32[576,128]{1,0:T(8,128)S(1)} %get-tuple-element.8), channel_id=1, source_target_pairs={{0,1},{1,0},{2,3},{3,2},{4,5},{5,4},{6,7},{7,6},{8,9},{9,8},{10,11... | collective-permute-start | bytes 884744 | tf_op jit(solution)/shard_map/ppermute | solution.py:18
  8.4 5.9 %collective-permute-start.1 = (f32[144,128]{1,0:T(8,128)S(1)}, f32[144,128]{1,0:T(8,128)S(1)}, u32[]{:S(2)}, u32[]{:S(2)}) collective-permute-start(f32[144,128]{1,0:T(8,128)S(1)} %get-tuple-element.9), channel_id=1, source_target_pairs={{0,7},{1,6},{2,5},{3,4},{4,3},{5,2},{6,1},{7,0},{8,15},{9,14},{10,... | collective-permute-start | bytes 221192 | tf_op jit(solution)/shard_map/ppermute | solution.py:18
  12.0 4.3 %collective-permute-start.3 = (f32[144,128]{1,0:T(8,128)S(1)}, f32[144,128]{1,0:T(8,128)S(1)}, u32[]{:S(2)}, u32[]{:S(2)}) collective-permute-start(f32[144,128]{1,0:T(8,128)S(1)} %get-tuple-element.10), channel_id=1, source_target_pairs={{0,5},{1,4},{2,7},{3,6},{4,1},{5,0},{6,3},{7,2},{8,13},{9,12},{10,... | collective-permute-start | bytes 221192 | tf_op jit(solution)/shard_map/ppermute | solution.py:18
  12.3 4.1 %collective-permute-start.2 = (f32[144,128]{1,0:T(8,128)S(1)}, f32[144,128]{1,0:T(8,128)S(1)}, u32[]{:S(2)}, u32[]{:S(2)}) collective-permute-start(f32[144,128]{1,0:T(8,128)S(1)} %get-tuple-element.11), channel_id=1, source_target_pairs={{0,2},{1,3},{2,0},{3,1},{4,6},{5,7},{6,4},{7,5},{8,10},{9,11},{10,... | collective-permute-start | bytes 221192 | tf_op jit(solution)/shard_map/ppermute | solution.py:18
  16.4 5.7 %collective-permute-start.4 = (f32[48,128]{1,0:T(8,128)S(1)}, f32[48,128]{1,0:T(8,128)S(1)}, u32[]{:S(2)}, u32[]{:S(2)}) collective-permute-start(f32[48,128]{1,0:T(8,128)S(1)} %get-tuple-element.15), channel_id=1, source_target_pairs={{0,25},{1,24},{2,27},{3,26},{4,29},{5,28},{6,31},{7,30},{8,17},{9,... | collective-permute-start | bytes 73736 | tf_op jit(solution)/shard_map/ppermute | solution.py:18
  20.4 2.7 %collective-permute-start.6 = (f32[48,128]{1,0:T(8,128)S(1)}, f32[48,128]{1,0:T(8,128)S(1)}, u32[]{:S(2)}, u32[]{:S(2)}) collective-permute-start(f32[48,128]{1,0:T(8,128)S(1)} %get-tuple-element.16), channel_id=1, source_target_pairs={{0,8},{1,9},{2,10},{3,11},{4,12},{5,13},{6,14},{7,15},{8,0},{9,1},... | collective-permute-start | bytes 73736 | tf_op jit(solution)/shard_map/ppermute | solution.py:18
  20.4 4.2 %collective-permute-start.5 = (f32[48,128]{1,0:T(8,128)S(1)}, f32[48,128]{1,0:T(8,128)S(1)}, u32[]{:S(2)}, u32[]{:S(2)}) collective-permute-start(f32[48,128]{1,0:T(8,128)S(1)} %get-tuple-element.17), channel_id=1, source_target_pairs={{0,17},{1,16},{2,19},{3,18},{4,21},{5,20},{6,23},{7,22},{8,25},{9,... | collective-permute-start | bytes 73736 | tf_op jit(solution)/shard_map/ppermute | solution.py:18

commit v2 on v1

--- a/solution.py
+++ b/solution.py
@@ -11,7 +11,7 @@
 CORE, X, Y, Z1, Z2 = 1, 2, 4, 8, 16
 PLANE = (X | Y | CORE, X, Y | CORE)
 LINE = (Z1 | Z2 | CORE, Z2 | CORE, Z1)
-CHUNKS = 4
+CHUNKS = 2
 
 
 def swap(value, mask):
@@ -35,17 +35,11 @@
     for copy in copies:
         copy.start()
     masks.start()
-    for k in range(CHUNKS):
-        copies[2 * k].wait()
-        copies[2 * k + 1].wait()
-        here = pl.ds(k * step, step)
-        term = lax.dot_general(
-            ground[here, :], response[here, :], (((0,), (0,)), ((), ())), preferred_element_type=jnp.float32
-        )
-        if k == 0:
-            product[...] = term
-        else:
-            product[...] += term
+    for copy in copies:
+        copy.wait()
+    product[...] = lax.dot_general(
+        ground[...], response[...], (((0,), (0,)), ((), ())), preferred_element_type=jnp.float32
+    )
     masks.wait()
 
     for i in range(nblocks):
@@ -82,12 +76,13 @@
     nocc_dev, aux_dev, nbasis = factors.shape
     depth = nocc_dev * aux_dev
     rows, cols = nbasis // 8, nbasis // 4
-    part = cols // 3
+    ground_rows = factors.reshape(depth, nbasis)
+    response_rows = response.reshape(depth, nbasis)
     half = jax.ShapeDtypeStruct((12 * rows, 128), jnp.float32)
     away, stay = pl.pallas_call(
         pack_kernel,
         out_shape=(half, half),
-        in_specs=[pl.BlockSpec(memory_space=pl.ANY)] * 3,
+        in_specs=[pl.BlockSpec(memory_space=pltpu.HBM)] * 3,
         out_specs=(pl.BlockSpec(memory_space=pltpu.VMEM),) * 2,
         scratch_shapes=[
             pltpu.VMEM((depth, nbasis), jnp.bfloat16),
@@ -98,7 +93,7 @@
             pltpu.SemaphoreType.DMA((2 * CHUNKS + 1,)),
         ],
         compiler_params=pltpu.CompilerParams(vmem_limit_bytes=32 * 1024 * 1024),
-    )(pattern, factors.reshape(depth, nbasis), response.reshape(depth, nbasis))
+    )(*(pltpu.with_memory_space_constraint(a, pltpu.HBM) for a in (pattern, ground_rows, response_rows)))
     chip = (stay + swap(away, CORE)).reshape(4, 3 * rows, 128)
     order = {X: 1, Y | CORE: 2, X | Y | CORE: 3}
     plane = [swap(chip[order[mask]], mask) for mask in PLANE]

time: 25.4 us -> 21.5 us (0.85)
  local copies, waits for them, and re-layouts: 3.05 us -> 0.1 us
  Pallas kernels: 3.71 us -> 2.81 us
    unnamed x6 -> x0, local copies, waits for them, and re-layouts: 2.95 us -> none
    pallas_call x1, Pallas kernels: 3.71 us -> 2.81 us  [fast_shards(): pl.pallas_call(pack_kernel, out_shape=(half, half), in_specs=[pl.BlockSpe...]
where the time goes in v2:
time: 21.5 us; the launch traced here: 21.4 us
  waiting for transfers between devices  8.91 us (41%)
  starting transfers between devices  8.75 us (41%)
  Pallas kernels  2.81 us (13%)
  other arithmetic  0.76 us (4%)
    ppermute x7, waiting for transfers between devices, swap(): return lax.ppermute(value, BOTH, [(i, i ^ mask) for i in range(32)])  8.91 us
    ppermute x7, starting transfers between devices, swap(): return lax.ppermute(value, BOTH, [(i, i ^ mask) for i in range(32)])  8.75 us
    pallas_call x1, Pallas kernels, fast_shards(): pl.pallas_call(pack_kernel, out_shape=(half, half), in_specs=[pl.BlockSpe...  2.81 us
    add x1, other arithmetic, fast_shards(): return own + last[0][:, :cols] + last[1][:, :cols] + last[2][:, :cols]  0.7 us
  transfers between devices with their start and end apart: 7, of which 6 were waited for; matrix products, arithmetic and copies ran while one was open for 0% of the time, Pallas kernels for 0%

profile of v2, /device:TPU:1, one launch (start us, length us, event | category | flops | bytes accessed | tf_op | source)
XLA Modules:
  0.0 21.4 jit_solution(4534825688335023798)
XLA Ops:
  0.0 2.8 %shard_map.37 = (f32[576,128]{1,0:T(8,128)S(1)}, f32[576,128]{1,0:T(8,128)S(1)}) custom-call(s32[3,3]{1,0:T(4,128)} %pattern_hbm.1, bf16[1024,384]{1,0:T(8,128)(2,1)} %bitcast.9, bf16[1024,384]{1,0:T(8,128)(2,1)} %bitcast.10), custom_call_target="tpu_custom_call" | custom-call | tf_op jit(solution)/shard_map/pallas_call | solution.py:82
  2.8 0.1 collective-permute-start
  2.9 1.5 %collective-permute-done = f32[576,128]{1,0:T(8,128)S(1)} collective-permute-done((f32[576,128]{1,0:T(8,128)S(1)}, f32[576,128]{1,0:T(8,128)S(1)}, u32[]{:S(2)}, u32[]{:S(2)}) %collective-permute-start) | collective-permute-done | bytes 294944 | tf_op jit(solution)/shard_map/ppermute | solution.py:18
  4.5 3.6 %collective-permute-start.1 = (f32[144,128]{1,0:T(8,128)S(1)}, f32[144,128]{1,0:T(8,128)S(1)}, u32[]{:S(2)}, u32[]{:S(2)}) collective-permute-start(f32[144,128]{1,0:T(8,128)S(1)} %get-tuple-element.9), channel_id=1, source_target_pairs={{0,7},{1,6},{2,5},{3,4},{4,3},{5,2},{6,1},{7,0},{8,15},{9,14},{10,... | collective-permute-start | bytes 221192 | tf_op jit(solution)/shard_map/ppermute | solution.py:18
  8.2 0.3 %collective-permute-start.3 = (f32[144,128]{1,0:T(8,128)S(1)}, f32[144,128]{1,0:T(8,128)S(1)}, u32[]{:S(2)}, u32[]{:S(2)}) collective-permute-start(f32[144,128]{1,0:T(8,128)S(1)} %get-tuple-element.10), channel_id=1, source_target_pairs={{0,5},{1,4},{2,7},{3,6},{4,1},{5,0},{6,3},{7,2},{8,13},{9,12},{10,... | collective-permute-start | bytes 221192 | tf_op jit(solution)/shard_map/ppermute | solution.py:18
  8.4 0.1 collective-permute-start.2
  8.5 1.9 %collective-permute-done.1 = f32[144,128]{1,0:T(8,128)S(1)} collective-permute-done((f32[144,128]{1,0:T(8,128)S(1)}, f32[144,128]{1,0:T(8,128)S(1)}, u32[]{:S(2)}, u32[]{:S(2)}) %collective-permute-start.1) | collective-permute-done | bytes 73760 | tf_op jit(solution)/shard_map/ppermute | solution.py:18
  10.4 2.0 %collective-permute-done.3 = f32[144,128]{1,0:T(8,128)S(1)} collective-permute-done((f32[144,128]{1,0:T(8,128)S(1)}, f32[144,128]{1,0:T(8,128)S(1)}, u32[]{:S(2)}, u32[]{:S(2)}) %collective-permute-start.3) | collective-permute-done | bytes 73760 | tf_op jit(solution)/shard_map/ppermute | solution.py:18
  12.5 0.0 collective-permute-done.2
  12.5 4.0 %collective-permute-start.4 = (f32[48,128]{1,0:T(8,128)S(1)}, f32[48,128]{1,0:T(8,128)S(1)}, u32[]{:S(2)}, u32[]{:S(2)}) collective-permute-start(f32[48,128]{1,0:T(8,128)S(1)} %get-tuple-element.15), channel_id=1, source_target_pairs={{0,25},{1,24},{2,27},{3,26},{4,29},{5,28},{6,31},{7,30},{8,17},{9,... | collective-permute-start | bytes 73736 | tf_op jit(solution)/shard_map/ppermute | solution.py:18
  16.5 0.0 collective-permute-start.6
  16.5 0.6 %collective-permute-start.5 = (f32[48,128]{1,0:T(8,128)S(1)}, f32[48,128]{1,0:T(8,128)S(1)}, u32[]{:S(2)}, u32[]{:S(2)}) collective-permute-start(f32[48,128]{1,0:T(8,128)S(1)} %get-tuple-element.17), channel_id=1, source_target_pairs={{0,17},{1,16},{2,19},{3,18},{4,21},{5,20},{6,23},{7,22},{8,25},{9,... | collective-permute-start | bytes 73736 | tf_op jit(solution)/shard_map/ppermute | solution.py:18
  17.2 0.1 slice_bitcast_fusion.2
  17.2 1.0 %collective-permute-done.4 = f32[48,128]{1,0:T(8,128)S(1)} collective-permute-done((f32[48,128]{1,0:T(8,128)S(1)}, f32[48,128]{1,0:T(8,128)S(1)}, u32[]{:S(2)}, u32[]{:S(2)}) %collective-permute-start.4) | collective-permute-done | bytes 24608 | tf_op jit(solution)/shard_map/ppermute | solution.py:18
  18.3 0.9 %collective-permute-done.6 = f32[48,128]{1,0:T(8,128)S(1)} collective-permute-done((f32[48,128]{1,0:T(8,128)S(1)}, f32[48,128]{1,0:T(8,128)S(1)}, u32[]{:S(2)}, u32[]{:S(2)}) %collective-permute-start.6) | collective-permute-done | bytes 24608 | tf_op jit(solution)/shard_map/ppermute | solution.py:18
  19.2 1.5 %collective-permute-done.5 = f32[48,128]{1,0:T(8,128)S(1)} collective-permute-done((f32[48,128]{1,0:T(8,128)S(1)}, f32[48,128]{1,0:T(8,128)S(1)}, u32[]{:S(2)}, u32[]{:S(2)}) %collective-permute-start.5) | collective-permute-done | bytes 24608 | tf_op jit(solution)/shard_map/ppermute | solution.py:18
  20.7 0.7 %slice_add_fusion.1 = f32[48,96]{1,0:T(8,128)} fusion(f32[48,128]{1,0:T(8,128)S(1)} %collective-permute-done.6, f32[48,128]{1,0:T(8,128)S(1)} %collective-permute-done.5, f32[48,128]{1,0:T(8,128)S(1)} %collective-permute-done.4, f32[48,32]{1,0:T(8,128)S(1)} %get-tuple-element.13, f32[48,32]{1,0:T(8,128)S(1)} %get-tuple-element.14, ...), kind=kLoop, calls=%fused_computation.3 | loop fusion | flops 23040 | bytes 92160 | tf_op jit(solution)/shard_map/add | solution.py:104
  (4 shorter events, 0.1 us)
Async XLA Ops:
  2.8 1.6 %collective-permute-start = (f32[576,128]{1,0:T(8,128)S(1)}, f32[576,128]{1,0:T(8,128)S(1)}, u32[]{:S(2)}, u32[]{:S(2)}) collective-permute-start(f32[576,128]{1,0:T(8,128)S(1)} %get-tuple-element.8), channel_id=1, source_target_pairs={{0,1},{1,0},{2,3},{3,2},{4,5},{5,4},{6,7},{7,6},{8,9},{9,8},{10,11... | collective-permute-start | bytes 884744 | tf_op jit(solution)/shard_map/ppermute | solution.py:18
  4.5 5.9 %collective-permute-start.1 = (f32[144,128]{1,0:T(8,128)S(1)}, f32[144,128]{1,0:T(8,128)S(1)}, u32[]{:S(2)}, u32[]{:S(2)}) collective-permute-start(f32[144,128]{1,0:T(8,128)S(1)} %get-tuple-element.9), channel_id=1, source_target_pairs={{0,7},{1,6},{2,5},{3,4},{4,3},{5,2},{6,1},{7,0},{8,15},{9,14},{10,... | collective-permute-start | bytes 221192 | tf_op jit(solution)/shard_map/ppermute | solution.py:18
  8.2 4.3 %collective-permute-start.3 = (f32[144,128]{1,0:T(8,128)S(1)}, f32[144,128]{1,0:T(8,128)S(1)}, u32[]{:S(2)}, u32[]{:S(2)}) collective-permute-start(f32[144,128]{1,0:T(8,128)S(1)} %get-tuple-element.10), channel_id=1, source_target_pairs={{0,5},{1,4},{2,7},{3,6},{4,1},{5,0},{6,3},{7,2},{8,13},{9,12},{10,... | collective-permute-start | bytes 221192 | tf_op jit(solution)/shard_map/ppermute | solution.py:18
  8.4 4.1 %collective-permute-start.2 = (f32[144,128]{1,0:T(8,128)S(1)}, f32[144,128]{1,0:T(8,128)S(1)}, u32[]{:S(2)}, u32[]{:S(2)}) collective-permute-start(f32[144,128]{1,0:T(8,128)S(1)} %get-tuple-element.11), channel_id=1, source_target_pairs={{0,2},{1,3},{2,0},{3,1},{4,6},{5,7},{6,4},{7,5},{8,10},{9,11},{10,... | collective-permute-start | bytes 221192 | tf_op jit(solution)/shard_map/ppermute | solution.py:18
  12.5 5.7 %collective-permute-start.4 = (f32[48,128]{1,0:T(8,128)S(1)}, f32[48,128]{1,0:T(8,128)S(1)}, u32[]{:S(2)}, u32[]{:S(2)}) collective-permute-start(f32[48,128]{1,0:T(8,128)S(1)} %get-tuple-element.15), channel_id=1, source_target_pairs={{0,25},{1,24},{2,27},{3,26},{4,29},{5,28},{6,31},{7,30},{8,17},{9,... | collective-permute-start | bytes 73736 | tf_op jit(solution)/shard_map/ppermute | solution.py:18
  16.5 2.7 %collective-permute-start.6 = (f32[48,128]{1,0:T(8,128)S(1)}, f32[48,128]{1,0:T(8,128)S(1)}, u32[]{:S(2)}, u32[]{:S(2)}) collective-permute-start(f32[48,128]{1,0:T(8,128)S(1)} %get-tuple-element.16), channel_id=1, source_target_pairs={{0,8},{1,9},{2,10},{3,11},{4,12},{5,13},{6,14},{7,15},{8,0},{9,1},... | collective-permute-start | bytes 73736 | tf_op jit(solution)/shard_map/ppermute | solution.py:18
  16.5 4.2 %collective-permute-start.5 = (f32[48,128]{1,0:T(8,128)S(1)}, f32[48,128]{1,0:T(8,128)S(1)}, u32[]{:S(2)}, u32[]{:S(2)}) collective-permute-start(f32[48,128]{1,0:T(8,128)S(1)} %get-tuple-element.17), channel_id=1, source_target_pairs={{0,17},{1,16},{2,19},{3,18},{4,21},{5,20},{6,23},{7,22},{8,25},{9,... | collective-permute-start | bytes 73736 | tf_op jit(solution)/shard_map/ppermute | solution.py:18

commit v3 on v2

v3 whole, which is shorter than its diff:
```python
import functools

import jax
import jax.numpy as jnp
from jax import lax
from jax.experimental import pallas as pl
from jax.experimental.pallas import tpu as pltpu
from jax.sharding import PartitionSpec as P

BOTH = ("aux", "occ")
FLIPS = (((0, 0, 1, 1), (0, 1, 0, 0)), ((1, 0, 1, 0), (1, 1, 0, 0)))
FLIP_BITS = sum(FLIPS[x][y][z] << (x * 8 + y * 4 + z) for x in range(2) for y in range(2) for z in range(4))
PLANE = ((1, 0, 0), (0, 1, 0), (1, 1, 0))
LINE = ((0, 0, 2), (0, 0, 1), (0, 0, 3))


def pairs(move):
    if move is None:
        return [(i, i ^ 1) for i in range(32)]
    found = []
    for i in range(32):
        x, y, z, core = i >> 1 & 1, i >> 2 & 1, i >> 3, i & 1
        kind = core ^ FLIPS[x][y][z]
        x, y, z = x ^ move[0], y ^ move[1], z ^ move[2]
        found.append((i, ((z * 2 + y) * 2 + x) * 2 + (kind ^ FLIPS[x][y][z])))
    return found


def swap(value, move):
    return lax.ppermute(value, BOTH, pairs(move))


def place():
    aux, occ = lax.axis_index("aux"), lax.axis_index("occ")
    return occ // 2, aux % 2, aux // 2, occ % 2


def product_kernel(pattern_hbm, ground_hbm, response_hbm, away_ref, stay_ref, ground, response, pattern, product, sems):
    nbasis = ground.shape[1]
    nblocks = pattern.shape[0]
    blk = nbasis // nblocks
    rows, cols = nbasis // 8, nbasis // 4

    copies = (
        pltpu.make_async_copy(ground_hbm, ground, sems.at[0]),
        pltpu.make_async_copy(response_hbm, response, sems.at[1]),
        pltpu.make_async_copy(pattern_hbm, pattern, sems.at[2]),
    )
    for copy in copies:
        copy.start()
    x, y, z, core = place()
    kind = core ^ (FLIP_BITS >> (x * 8 + y * 4 + z)) & 1
    for copy in copies:
        copy.wait()
    product[...] = lax.dot_general(
        ground[...], response[...], (((0,), (0,)), ((), ())), preferred_element_type=jnp.float32
    )
    for i in range(nblocks):
        for j in range(i, nblocks):
            upper = 0.5 * pattern[i, j].astype(jnp.float32)
            lower = 0.5 * pattern[j, i].astype(jnp.float32)
            at_i, at_j = slice(i * blk, (i + 1) * blk), slice(j * blk, (j + 1) * blk)
            both = upper * product[at_i, at_j] + lower * product[at_j, at_i].T
            product[at_i, at_j] = both
            if i != j:
                product[at_j, at_i] = both.T

    lane = lax.broadcasted_iota(jnp.int32, (rows, nbasis), 1)
    even = sum(((lane >= rows * k).astype(jnp.int32) for k in range(1, 8))) & 1 == 0
    z_to = sum((lane >= cols * k).astype(jnp.int32) for k in range(1, 4))
    for turn in range(2):
        x_to = x ^ turn
        base = pl.multiple_of(2 * cols * x_to, 8)
        upper, lower = ([product[pl.ds(base + cols * c + at, rows), :] for c in range(2)] for at in (0, rows))
        for y_to in range(2):
            if y_to == 0:
                tiles = [jnp.where(even, u, pltpu.roll(d, rows, 1)) for u, d in zip(upper, lower)]
            else:
                tiles = [jnp.where(even, pltpu.roll(u, nbasis - rows, 1), d) for u, d in zip(upper, lower)]
            flips = lax.shift_right_logical(jnp.full_like(z_to, FLIP_BITS), x_to * 8 + y_to * 4 + z_to) & 1
            other = (flips ^ kind) == 0
            group = turn + 2 * (y ^ y_to)
            away_ref[group, :, :] = jnp.where(other, tiles[1], tiles[0])
            stay_ref[group, :, :] = jnp.where(other, tiles[0], tiles[1])


def split_kernel(own_ref, a_ref, b_ref, c_ref, out_ref):
    cols = own_ref.shape[1] // 4
    total = own_ref[...] + a_ref[...] + b_ref[...] + c_ref[...]
    x, y, z, core = place()
    for z_to in range(4):
        out_ref[z ^ z_to, :, :cols] = total[:, cols * z_to : cols * (z_to + 1)]


def turn_kernel(own_ref, a_ref, b_ref, c_ref, out_ref):
    rows, cols = out_ref.shape
    total = own_ref[...] + a_ref[...] + b_ref[...] + c_ref[...]
    turned = total[:, :cols].T
    out_ref[...] = jnp.concatenate([turned[:rows], turned[rows:]], axis=1)


def fast_shards(factors, response, pattern):
    nocc_dev, aux_dev, nbasis = factors.shape
    depth = nocc_dev * aux_dev
    rows, cols = nbasis // 8, nbasis // 4
    vmem = pl.BlockSpec(memory_space=pltpu.VMEM)
    params = pltpu.CompilerParams(vmem_limit_bytes=32 * 1024 * 1024)
    half = jax.ShapeDtypeStruct((4, rows, nbasis), jnp.float32)
    inputs = (pattern, factors.reshape(depth, nbasis), response.reshape(depth, nbasis))
    away, stay = pl.pallas_call(
        product_kernel,
        out_shape=(half, half),
        in_specs=[pl.BlockSpec(memory_space=pl.ANY)] * 3,
        out_specs=(vmem, vmem),
        scratch_shapes=[
            pltpu.VMEM((depth, nbasis), jnp.bfloat16),
            pltpu.VMEM((depth, nbasis), jnp.bfloat16),
            pltpu.SMEM(pattern.shape, jnp.int32),
            pltpu.VMEM((nbasis, nbasis), jnp.float32),
            pltpu.SemaphoreType.DMA((3,)),
        ],
        compiler_params=params,
    )(*(pltpu.with_memory_space_constraint(a, pltpu.HBM) for a in inputs))
    chip = stay + swap(away, None)
    plane = [swap(chip[move[0] + 2 * move[1]], move) for move in PLANE]
    line = pl.pallas_call(
        split_kernel,
        out_shape=jax.ShapeDtypeStruct((4, rows, 128), jnp.float32),
        in_specs=[vmem] * 4,
        out_specs=vmem,
        compiler_params=params,
    )(chip[0], *plane)
    last = [swap(line[move[2]], move) for move in LINE]
    return pl.pallas_call(
        turn_kernel,
        out_shape=jax.ShapeDtypeStruct((rows, cols), jnp.float32),
        in_specs=[vmem] * 4,
        out_specs=vmem,
        compiler_params=params,
    )(line[0], *last)


def any_shards(factors, response, pattern):
    nocc_dev, aux_dev, nbasis = factors.shape
    ground_rows = factors.reshape(nocc_dev * aux_dev, nbasis)
    response_rows = response.reshape(nocc_dev * aux_dev, nbasis)
    blk = nbasis // pattern.shape[0]
    own_cols = nbasis // lax.axis_size("occ")
    cross = lax.dot_general(
        ground_rows, response_rows, (((0,), (0,)), ((), ())), preferred_element_type=jnp.float32
    )
    masked = jnp.repeat(jnp.repeat(pattern.astype(jnp.float32), blk, axis=0), blk, axis=1) * cross
    both = 0.5 * (masked + masked.T)
    own_rows = lax.psum_scatter(both, "aux", scatter_dimension=0, tiled=True)
    summed = lax.psum(own_rows, "occ")
    return lax.dynamic_slice_in_dim(summed, lax.axis_index("occ") * own_cols, own_cols, 1)


def solution(mesh):
    in_specs = (P("occ", "aux", None), P("occ", "aux", None), P())
    out_specs = P("aux", "occ")
    sizes = dict(mesh.shape)
    shards = fast_shards if sizes["aux"] == 8 and sizes["occ"] == 4 else any_shards
    return jax.shard_map(shards, mesh=mesh, in_specs=in_specs, out_specs=out_specs, check_vma=False)
```

time: 21.5 us -> 21 us (0.977)
  other arithmetic: 0.76 us -> 0.04 us
  Pallas kernels: 2.81 us -> 3.29 us
    add x3 -> x1, other arithmetic: 0.76 us -> 0.04 us  [fast_shards(): chip = stay + swap(away, None)]
    pallas_call x1 -> x3, Pallas kernels: 2.81 us -> 3.29 us  [the longest x1 2.42 us: fast_shards(): pl.pallas_call(product_kernel, out_shape=(half, half), in_specs=[pl.Block...]
  transfers between devices with their start and end apart: 7 -> 7, of which waited for: 6 -> 7; matrix products, arithmetic and copies ran while one was open for 0% -> 0% of each run, Pallas kernels for 0% -> 0%
where the time goes in v3:
time: 21 us; the launch traced here: 20.9 us
  waiting for transfers between devices  8.9 us (42%)
  starting transfers between devices  8.56 us (41%)
  Pallas kernels  3.29 us (16%)
    ppermute x7, waiting for transfers between devices, swap(): return lax.ppermute(value, BOTH, pairs(move))  8.9 us
    ppermute x7, starting transfers between devices, swap(): return lax.ppermute(value, BOTH, pairs(move))  8.56 us
    pallas_call x1, Pallas kernels, fast_shards(): pl.pallas_call(product_kernel, out_shape=(half, half), in_specs=[pl.Block...  2.42 us
    pallas_call x1, Pallas kernels, fast_shards(): pl.pallas_call(turn_kernel, out_shape=jax.ShapeDtypeStruct((rows, cols),...  0.77 us
  transfers between devices with their start and end apart: 7, of which 7 were waited for; matrix products, arithmetic and copies ran while one was open for 0% of the time, Pallas kernels for 0%

profile of v3, /device:TPU:1, one launch (start us, length us, event | category | flops | bytes accessed | tf_op | source)
XLA Modules:
  0.0 20.9 jit_solution(16721751018310651864)
XLA Ops:
  0.0 2.4 %shard_map.37 = (f32[4,48,384]{2,1,0:T(8,128)S(1)}, f32[4,48,384]{2,1,0:T(8,128)S(1)}) custom-call(s32[3,3]{1,0:T(4,128)} %pattern_hbm.1, bf16[1024,384]{1,0:T(8,128)(2,1)} %bitcast.18, bf16[1024,384]{1,0:T(8,128)(2,1)} %bitcast.19), custom_call_target="tpu_custom_call" | custom-call | tf_op jit(solution)/shard_map/pallas_call | solution.py:110
  2.4 0.1 collective-permute-start
  2.6 1.5 %collective-permute-done = f32[4,48,384]{2,1,0:T(8,128)S(1)} collective-permute-done((f32[4,48,384]{2,1,0:T(8,128)S(1)}, f32[4,48,384]{2,1,0:T(8,128)S(1)}, u32[]{:S(2)}, u32[]{:S(2)}) %collective-permute-start) | collective-permute-done | bytes 294944 | tf_op jit(solution)/shard_map/ppermute | solution.py:30
  4.1 3.6 %collective-permute-start.3 = (f32[48,384]{1,0:T(8,128)S(1)}, f32[48,384]{1,0:T(8,128)S(1)}, u32[]{:S(2)}, u32[]{:S(2)}) collective-permute-start(f32[48,384]{1,0:T(8,128)S(1)} %get-tuple-element.9), channel_id=1, source_target_pairs={{0,7},{1,6},{2,5},{3,4},{4,3},{5,2},{6,1},{7,0},{8,15},{9,14},{10,... | collective-permute-start | bytes 221192 | tf_op jit(solution)/shard_map/ppermute | solution.py:30
  7.8 0.2 %collective-permute-start.2 = (f32[48,384]{1,0:T(8,128)S(1)}, f32[48,384]{1,0:T(8,128)S(1)}, u32[]{:S(2)}, u32[]{:S(2)}) collective-permute-start(f32[48,384]{1,0:T(8,128)S(1)} %get-tuple-element.10), channel_id=1, source_target_pairs={{0,4},{1,5},{2,6},{3,7},{4,0},{5,1},{6,2},{7,3},{8,13},{9,12},{10,... | collective-permute-start | bytes 221192 | tf_op jit(solution)/shard_map/ppermute | solution.py:30
  8.0 0.4 %collective-permute-start.1 = (f32[48,384]{1,0:T(8,128)S(1)}, f32[48,384]{1,0:T(8,128)S(1)}, u32[]{:S(2)}, u32[]{:S(2)}) collective-permute-start(f32[48,384]{1,0:T(8,128)S(1)} %get-tuple-element.11), channel_id=1, source_target_pairs={{0,3},{1,2},{2,1},{3,0},{4,7},{5,6},{6,5},{7,4},{8,10},{9,11},{10,... | collective-permute-start | bytes 221192 | tf_op jit(solution)/shard_map/ppermute | solution.py:30
  8.4 1.6 %collective-permute-done.3.c_ref = f32[48,384]{1,0:T(8,128)S(1)} collective-permute-done((f32[48,384]{1,0:T(8,128)S(1)}, f32[48,384]{1,0:T(8,128)S(1)}, u32[]{:S(2)}, u32[]{:S(2)}) %collective-permute-start.3) | collective-permute-done | bytes 73760 | tf_op jit(solution)/shard_map/ppermute | solution.py:30
  10.0 1.5 %collective-permute-done.2.b_ref = f32[48,384]{1,0:T(8,128)S(1)} collective-permute-done((f32[48,384]{1,0:T(8,128)S(1)}, f32[48,384]{1,0:T(8,128)S(1)}, u32[]{:S(2)}, u32[]{:S(2)}) %collective-permute-start.2) | collective-permute-done | bytes 73760 | tf_op jit(solution)/shard_map/ppermute | solution.py:30
  11.5 0.8 %collective-permute-done.1.a_ref = f32[48,384]{1,0:T(8,128)S(1)} collective-permute-done((f32[48,384]{1,0:T(8,128)S(1)}, f32[48,384]{1,0:T(8,128)S(1)}, u32[]{:S(2)}, u32[]{:S(2)}) %collective-permute-start.1) | collective-permute-done | bytes 73760 | tf_op jit(solution)/shard_map/ppermute | solution.py:30
  12.3 0.1 shard_map.38
  12.5 3.4 %collective-permute-start.6 = (f32[48,128]{1,0:T(8,128)S(1)}, f32[48,128]{1,0:T(8,128)S(1)}, u32[]{:S(2)}, u32[]{:S(2)}) collective-permute-start(f32[48,128]{1,0:T(8,128)S(1)} %get-tuple-element.13), channel_id=1, source_target_pairs={{0,25},{1,24},{2,27},{3,26},{4,28},{5,29},{6,31},{7,30},{8,17},{9,... | collective-permute-start | bytes 73736 | tf_op jit(solution)/shard_map/ppermute | solution.py:30
  15.9 0.0 collective-permute-start.5
  15.9 0.7 %collective-permute-start.4 = (f32[48,128]{1,0:T(8,128)S(1)}, f32[48,128]{1,0:T(8,128)S(1)}, u32[]{:S(2)}, u32[]{:S(2)}) collective-permute-start(f32[48,128]{1,0:T(8,128)S(1)} %get-tuple-element.15), channel_id=1, source_target_pairs={{0,17},{1,16},{2,18},{3,19},{4,20},{5,21},{6,23},{7,22},{8,25},{9,... | collective-permute-start | bytes 73736 | tf_op jit(solution)/shard_map/ppermute | solution.py:30
  16.6 1.0 %collective-permute-done.6.c_ref = f32[48,128]{1,0:T(8,128)S(1)} collective-permute-done((f32[48,128]{1,0:T(8,128)S(1)}, f32[48,128]{1,0:T(8,128)S(1)}, u32[]{:S(2)}, u32[]{:S(2)}) %collective-permute-start.6) | collective-permute-done | bytes 24608 | tf_op jit(solution)/shard_map/ppermute | solution.py:30
  17.7 1.0 %collective-permute-done.5.b_ref = f32[48,128]{1,0:T(8,128)S(1)} collective-permute-done((f32[48,128]{1,0:T(8,128)S(1)}, f32[48,128]{1,0:T(8,128)S(1)}, u32[]{:S(2)}, u32[]{:S(2)}) %collective-permute-start.5) | collective-permute-done | bytes 24608 | tf_op jit(solution)/shard_map/ppermute | solution.py:30
  18.6 1.5 %collective-permute-done.4.a_ref = f32[48,128]{1,0:T(8,128)S(1)} collective-permute-done((f32[48,128]{1,0:T(8,128)S(1)}, f32[48,128]{1,0:T(8,128)S(1)}, u32[]{:S(2)}, u32[]{:S(2)}) %collective-permute-start.4) | collective-permute-done | bytes 24608 | tf_op jit(solution)/shard_map/ppermute | solution.py:30
  20.1 0.8 %shard_map.39 = f32[48,96]{1,0:T(8,128)} custom-call(f32[48,128]{1,0:T(8,128)S(1)} %get-tuple-element.16.own_ref, f32[48,128]{1,0:T(8,128)S(1)} %collective-permute-done.4.a_ref, f32[48,128]{1,0:T(8,128)S(1)} %collective-permute-done.5.b_ref, f32[48,128]{1,0:T(8,128)S(1)} %collective-permute-done.6.c_ref), custom_call_target="tpu_custom_call" | custom-call | tf_op jit(solution)/shard_map/pallas_call | solution.py:134
  (3 shorter events, 0.1 us)
Async XLA Ops:
  2.4 1.6 %collective-permute-start = (f32[4,48,384]{2,1,0:T(8,128)S(1)}, f32[4,48,384]{2,1,0:T(8,128)S(1)}, u32[]{:S(2)}, u32[]{:S(2)}) collective-permute-start(f32[4,48,384]{2,1,0:T(8,128)S(1)} %get-tuple-element.8), channel_id=1, source_target_pairs={{0,1},{1,0},{2,3},{3,2},{4,5},{5,4},{6,7},{7,6},{8,9},{9,8},{10,11... | collective-permute-start | bytes 884744 | tf_op jit(solution)/shard_map/ppermute | solution.py:30
  4.1 5.9 %collective-permute-start.3 = (f32[48,384]{1,0:T(8,128)S(1)}, f32[48,384]{1,0:T(8,128)S(1)}, u32[]{:S(2)}, u32[]{:S(2)}) collective-permute-start(f32[48,384]{1,0:T(8,128)S(1)} %get-tuple-element.9), channel_id=1, source_target_pairs={{0,7},{1,6},{2,5},{3,4},{4,3},{5,2},{6,1},{7,0},{8,15},{9,14},{10,... | collective-permute-start | bytes 221192 | tf_op jit(solution)/shard_map/ppermute | solution.py:30
  7.8 3.7 %collective-permute-start.2 = (f32[48,384]{1,0:T(8,128)S(1)}, f32[48,384]{1,0:T(8,128)S(1)}, u32[]{:S(2)}, u32[]{:S(2)}) collective-permute-start(f32[48,384]{1,0:T(8,128)S(1)} %get-tuple-element.10), channel_id=1, source_target_pairs={{0,4},{1,5},{2,6},{3,7},{4,0},{5,1},{6,2},{7,3},{8,13},{9,12},{10,... | collective-permute-start | bytes 221192 | tf_op jit(solution)/shard_map/ppermute | solution.py:30
  8.0 4.3 %collective-permute-start.1 = (f32[48,384]{1,0:T(8,128)S(1)}, f32[48,384]{1,0:T(8,128)S(1)}, u32[]{:S(2)}, u32[]{:S(2)}) collective-permute-start(f32[48,384]{1,0:T(8,128)S(1)} %get-tuple-element.11), channel_id=1, source_target_pairs={{0,3},{1,2},{2,1},{3,0},{4,7},{5,6},{6,5},{7,4},{8,10},{9,11},{10,... | collective-permute-start | bytes 221192 | tf_op jit(solution)/shard_map/ppermute | solution.py:30
  12.5 5.2 %collective-permute-start.6 = (f32[48,128]{1,0:T(8,128)S(1)}, f32[48,128]{1,0:T(8,128)S(1)}, u32[]{:S(2)}, u32[]{:S(2)}) collective-permute-start(f32[48,128]{1,0:T(8,128)S(1)} %get-tuple-element.13), channel_id=1, source_target_pairs={{0,25},{1,24},{2,27},{3,26},{4,28},{5,29},{6,31},{7,30},{8,17},{9,... | collective-permute-start | bytes 73736 | tf_op jit(solution)/shard_map/ppermute | solution.py:30
  15.9 2.7 %collective-permute-start.5 = (f32[48,128]{1,0:T(8,128)S(1)}, f32[48,128]{1,0:T(8,128)S(1)}, u32[]{:S(2)}, u32[]{:S(2)}) collective-permute-start(f32[48,128]{1,0:T(8,128)S(1)} %get-tuple-element.14), channel_id=1, source_target_pairs={{0,8},{1,9},{2,11},{3,10},{4,13},{5,12},{6,14},{7,15},{8,0},{9,1},... | collective-permute-start | bytes 73736 | tf_op jit(solution)/shard_map/ppermute | solution.py:30
  15.9 4.2 %collective-permute-start.4 = (f32[48,128]{1,0:T(8,128)S(1)}, f32[48,128]{1,0:T(8,128)S(1)}, u32[]{:S(2)}, u32[]{:S(2)}) collective-permute-start(f32[48,128]{1,0:T(8,128)S(1)} %get-tuple-element.15), channel_id=1, source_target_pairs={{0,17},{1,16},{2,18},{3,19},{4,20},{5,21},{6,23},{7,22},{8,25},{9,... | collective-permute-start | bytes 73736 | tf_op jit(solution)/shard_map/ppermute | solution.py:30

commit v4 on v3

--- a/solution.py
+++ b/solution.py
@@ -8,10 +8,10 @@
 from jax.sharding import PartitionSpec as P
 
 BOTH = ("aux", "occ")
-FLIPS = (((0, 0, 1, 1), (0, 1, 0, 0)), ((1, 0, 1, 0), (1, 1, 0, 0)))
+FLIPS = (((0, 1, 1, 1), (0, 1, 0, 0)), ((0, 0, 1, 0), (1, 1, 0, 0)))
 FLIP_BITS = sum(FLIPS[x][y][z] << (x * 8 + y * 4 + z) for x in range(2) for y in range(2) for z in range(4))
-PLANE = ((1, 0, 0), (0, 1, 0), (1, 1, 0))
-LINE = ((0, 0, 2), (0, 0, 1), (0, 0, 3))
+PLANE = ((1, 0, 0), (1, 1, 0))
+LINE = ((0, 0, 1), (0, 0, 2), (0, 0, 3))
 
 
 def pairs(move):
@@ -35,7 +35,7 @@
     return occ // 2, aux % 2, aux // 2, occ % 2
 
 
-def product_kernel(pattern_hbm, ground_hbm, response_hbm, away_ref, stay_ref, ground, response, pattern, product, sems):
+def product_kernel(pattern_hbm, ground_hbm, response_hbm, out_ref, ground, response, pattern, product, whole, turned, sems):
     nbasis = ground.shape[1]
     nblocks = pattern.shape[0]
     blk = nbasis // nblocks
@@ -50,20 +50,23 @@
         copy.start()
     x, y, z, core = place()
     kind = core ^ (FLIP_BITS >> (x * 8 + y * 4 + z)) & 1
-    for copy in copies:
-        copy.wait()
-    product[...] = lax.dot_general(
-        ground[...], response[...], (((0,), (0,)), ((), ())), preferred_element_type=jnp.float32
-    )
+    copies[0].wait()
+    turned[...] = ground[...].T
+    copies[1].wait()
+    copies[2].wait()
+    block = lax.dot_general(turned[0:128, :], response[...], (((1,), (0,)), ((), ())), preferred_element_type=jnp.float32)
+    for j in range(3):
+        product[0:128, 128 * j : 128 * j + 128] = 0.5 * pattern[0, j].astype(jnp.float32) * block[:, 128 * j : 128 * j + 128]
+    block = lax.dot_general(turned[128:256, :], response[...], (((1,), (0,)), ((), ())), preferred_element_type=jnp.float32)
+    for j in range(3):
+        product[128:256, 128 * j : 128 * j + 128] = 0.5 * pattern[1, j].astype(jnp.float32) * block[:, 128 * j : 128 * j + 128]
+    block = lax.dot_general(turned[256:384, :], response[...], (((1,), (0,)), ((), ())), preferred_element_type=jnp.float32)
+    for j in range(3):
+        product[256:384, 128 * j : 128 * j + 128] = 0.5 * pattern[2, j].astype(jnp.float32) * block[:, 128 * j : 128 * j + 128]
     for i in range(nblocks):
-        for j in range(i, nblocks):
-            upper = 0.5 * pattern[i, j].astype(jnp.float32)
-            lower = 0.5 * pattern[j, i].astype(jnp.float32)
+        for j in range(nblocks):
             at_i, at_j = slice(i * blk, (i + 1) * blk), slice(j * blk, (j + 1) * blk)
-            both = upper * product[at_i, at_j] + lower * product[at_j, at_i].T
-            product[at_i, at_j] = both
-            if i != j:
-                product[at_j, at_i] = both.T
+            whole[at_i, at_j] = product[at_i, at_j] + product[at_j, at_i].T
 
     lane = lax.broadcasted_iota(jnp.int32, (rows, nbasis), 1)
     even = sum(((lane >= rows * k).astype(jnp.int32) for k in range(1, 8))) & 1 == 0
@@ -71,7 +74,7 @@
     for turn in range(2):
         x_to = x ^ turn
         base = pl.multiple_of(2 * cols * x_to, 8)
-        upper, lower = ([product[pl.ds(base + cols * c + at, rows), :] for c in range(2)] for at in (0, rows))
+        upper, lower = ([whole[pl.ds(base + cols * c + at, rows), :] for c in range(2)] for at in (0, rows))
         for y_to in range(2):
             if y_to == 0:
                 tiles = [jnp.where(even, u, pltpu.roll(d, rows, 1)) for u, d in zip(upper, lower)]
@@ -79,9 +82,14 @@
                 tiles = [jnp.where(even, pltpu.roll(u, nbasis - rows, 1), d) for u, d in zip(upper, lower)]
             flips = lax.shift_right_logical(jnp.full_like(z_to, FLIP_BITS), x_to * 8 + y_to * 4 + z_to) & 1
             other = (flips ^ kind) == 0
-            group = turn + 2 * (y ^ y_to)
-            away_ref[group, :, :] = jnp.where(other, tiles[1], tiles[0])
-            stay_ref[group, :, :] = jnp.where(other, tiles[0], tiles[1])
+            stay, away = ((0, 6), (1, 6)) if turn == 0 else ((2, 1), (4, 1))
+            out_ref[stay[0] + stay[1] * (y ^ y_to), :, :] = jnp.where(other, tiles[0], tiles[1])
+            out_ref[away[0] + away[1] * (y ^ y_to), :, :] = jnp.where(other, tiles[1], tiles[0])
+
+
+def side_kernel(own_ref, came_ref, x_ref, y_ref):
+    x_ref[...] = own_ref[0] + came_ref[0]
+    y_ref[...] = own_ref[1] + came_ref[1]
 
 
 def split_kernel(own_ref, a_ref, b_ref, c_ref, out_ref):
@@ -105,31 +113,43 @@
     rows, cols = nbasis // 8, nbasis // 4
     vmem = pl.BlockSpec(memory_space=pltpu.VMEM)
     params = pltpu.CompilerParams(vmem_limit_bytes=32 * 1024 * 1024)
-    half = jax.ShapeDtypeStruct((4, rows, nbasis), jnp.float32)
     inputs = (pattern, factors.reshape(depth, nbasis), response.reshape(depth, nbasis))
-    away, stay = pl.pallas_call(
+    parts = pl.pallas_call(
         product_kernel,
-        out_shape=(half, half),
+        out_shape=jax.ShapeDtypeStruct((8, rows, nbasis), jnp.float32),
         in_specs=[pl.BlockSpec(memory_space=pl.ANY)] * 3,
-        out_specs=(vmem, vmem),
+        out_specs=vmem,
         scratch_shapes=[
             pltpu.VMEM((depth, nbasis), jnp.bfloat16),
             pltpu.VMEM((depth, nbasis), jnp.bfloat16),
             pltpu.SMEM(pattern.shape, jnp.int32),
             pltpu.VMEM((nbasis, nbasis), jnp.float32),
+            pltpu.VMEM((nbasis, nbasis), jnp.float32),
+            pltpu.VMEM((nbasis, depth), jnp.bfloat16),
             pltpu.SemaphoreType.DMA((3,)),
         ],
         compiler_params=params,
     )(*(pltpu.with_memory_space_constraint(a, pltpu.HBM) for a in inputs))
-    chip = stay + swap(away, None)
-    plane = [swap(chip[move[0] + 2 * move[1]], move) for move in PLANE]
+    side = jax.ShapeDtypeStruct((rows, nbasis), jnp.float32)
+    sides = pl.pallas_call(
+        side_kernel,
+        out_shape=(side, side),
+        in_specs=[vmem] * 2,
+        out_specs=(vmem, vmem),
+        cost_estimate=pl.CostEstimate(flops=100000, bytes_accessed=600000, transcendentals=0),
+        compiler_params=params,
+    )(parts[2:4], swap(parts[4:6], None))
+    far = swap(parts[6:8], (0, 1, 0))
+    near = [swap(sides[move[1]], move) for move in PLANE]
+    own = parts[0:2] + far
+    plane = [swap(own[1], None), *near]
     line = pl.pallas_call(
         split_kernel,
         out_shape=jax.ShapeDtypeStruct((4, rows, 128), jnp.float32),
         in_specs=[vmem] * 4,
         out_specs=vmem,
         compiler_params=params,
-    )(chip[0], *plane)
+    )(own[0], *plane)
     last = [swap(line[move[2]], move) for move in LINE]
     return pl.pallas_call(
         turn_kernel,

time: 21 us -> 20.6 us (0.981)
  waiting for transfers between devices: 8.9 us -> 6.87 us
  starting transfers between devices: 8.56 us -> 10.2 us
    ppermute x7 -> x8, waiting for transfers between devices: 8.9 us -> 6.87 us  [swap(): return lax.ppermute(value, BOTH, pairs(move))]
    ppermute x7 -> x8, starting transfers between devices: 8.56 us -> 10.2 us  [swap(): return lax.ppermute(value, BOTH, pairs(move))]
    pallas_call x1 -> x2, Pallas kernels: 2.42 us -> 2.35 us  [the longest x1 2.33 us: fast_shards(): pl.pallas_call(product_kernel, out_shape=jax.ShapeDtypeStruct((8, rows, n...]
  transfers between devices with their start and end apart: 7 -> 8, of which waited for: 7 -> 4; matrix products, arithmetic and copies ran while one was open for 0% -> 0% of each run, Pallas kernels for 0% -> 0%
where the time goes in v4:
time: 20.6 us; the launch traced here: 20.5 us
  starting transfers between devices  10.2 us (50%)
  waiting for transfers between devices  6.87 us (33%)
  Pallas kernels  3.22 us (16%)
    ppermute x8, starting transfers between devices, swap(): return lax.ppermute(value, BOTH, pairs(move))  10.2 us
    ppermute x8, waiting for transfers between devices, swap(): return lax.ppermute(value, BOTH, pairs(move))  6.87 us
    pallas_call x1, Pallas kernels, fast_shards(): pl.pallas_call(product_kernel, out_shape=jax.ShapeDtypeStruct((8, rows, n...  2.33 us
    pallas_call x1, Pallas kernels, fast_shards(): pl.pallas_call(turn_kernel, out_shape=jax.ShapeDtypeStruct((rows, cols),...  0.77 us
  transfers between devices with their start and end apart: 8, of which 4 were waited for; matrix products, arithmetic and copies ran while one was open for 0% of the time, Pallas kernels for 0%

profile of v4, /device:TPU:1, one launch (start us, length us, event | category | flops | bytes accessed | tf_op | source)
XLA Modules:
  0.0 20.5 jit_solution(12113838366112256849)
XLA Ops:
  0.0 2.3 %shard_map.37 = f32[8,48,384]{2,1,0:T(8,128)S(1)} custom-call(s32[3,3]{1,0:T(4,128)} %pattern_hbm.1, bf16[1024,384]{1,0:T(8,128)(2,1)} %bitcast.14, bf16[1024,384]{1,0:T(8,128)(2,1)} %bitcast.15), custom_call_target="tpu_custom_call" | custom-call | tf_op jit(solution)/shard_map/pallas_call | solution.py:117
  2.4 0.1 collective-permute-start.2
  2.5 2.7 %collective-permute-start = (f32[2,48,384]{2,1,0:T(8,128)S(1)}, f32[2,48,384]{2,1,0:T(8,128)S(1)}, u32[]{:S(2)}, u32[]{:S(2)}) collective-permute-start(f32[2,48,384]{2,1,0:T(8,128)S(1)} %get-tuple-element.11), channel_id=1, source_target_pairs={{0,4},{1,5},{2,7},{3,6},{4,0},{5,1},{6,3},{7,2},{8,12},{9,13},{10,... | collective-permute-start | bytes 442376 | tf_op jit(solution)/shard_map/ppermute | solution.py:30
  5.2 0.0 collective-permute-done.2.came_ref
  5.2 1.2 %collective-permute-start.3 = (f32[48,384]{1,0:T(8,128)S(1)}, f32[48,384]{1,0:T(8,128)S(1)}, u32[]{:S(2)}, u32[]{:S(2)}) collective-permute-start(f32[48,384]{1,0:T(8,128)S(1)} %get-tuple-element.7), channel_id=1, source_target_pairs={{0,2},{1,3},{2,0},{3,1},{4,7},{5,6},{6,5},{7,4},{8,11},{9,10},{10,... | collective-permute-start | bytes 221192 | tf_op jit(solution)/shard_map/ppermute | solution.py:30
  6.5 1.3 %collective-permute-start.4 = (f32[48,384]{1,0:T(8,128)S(1)}, f32[48,384]{1,0:T(8,128)S(1)}, u32[]{:S(2)}, u32[]{:S(2)}) collective-permute-start(f32[48,384]{1,0:T(8,128)S(1)} %get-tuple-element.8), channel_id=1, source_target_pairs={{0,7},{1,6},{2,4},{3,5},{4,2},{5,3},{6,1},{7,0},{8,14},{9,15},{10,... | collective-permute-start | bytes 221192 | tf_op jit(solution)/shard_map/ppermute | solution.py:30
  7.8 1.6 %collective-permute-done = f32[2,48,384]{2,1,0:T(8,128)S(1)} collective-permute-done((f32[2,48,384]{2,1,0:T(8,128)S(1)}, f32[2,48,384]{2,1,0:T(8,128)S(1)}, u32[]{:S(2)}, u32[]{:S(2)}) %collective-permute-start) | collective-permute-done | bytes 147488 | tf_op jit(solution)/shard_map/ppermute | solution.py:30
  9.4 0.7 %collective-permute-start.1 = (f32[48,384]{1,0:T(8,128)S(1)}, f32[48,384]{1,0:T(8,128)S(1)}, u32[]{:S(2)}, u32[]{:S(2)}) collective-permute-start(f32[48,384]{1,0:T(8,128)S(1)} %get-tuple-element.12), channel_id=1, source_target_pairs={{0,1},{1,0},{2,3},{3,2},{4,5},{5,4},{6,7},{7,6},{8,9},{9,8},{10,11... | collective-permute-start | bytes 221192 | tf_op jit(solution)/shard_map/ppermute | solution.py:30
  10.1 0.0 collective-permute-done.3.b_ref
  10.1 2.1 %collective-permute-done.4.c_ref = f32[48,384]{1,0:T(8,128)S(1)} collective-permute-done((f32[48,384]{1,0:T(8,128)S(1)}, f32[48,384]{1,0:T(8,128)S(1)}, u32[]{:S(2)}, u32[]{:S(2)}) %collective-permute-start.4) | collective-permute-done | bytes 73760 | tf_op jit(solution)/shard_map/ppermute | solution.py:30
  12.2 0.0 collective-permute-done.1.a_ref
  12.2 0.1 shard_map.39
  12.3 3.0 %collective-permute-start.7 = (f32[48,128]{1,0:T(8,128)S(1)}, f32[48,128]{1,0:T(8,128)S(1)}, u32[]{:S(2)}, u32[]{:S(2)}) collective-permute-start(f32[48,128]{1,0:T(8,128)S(1)} %get-tuple-element.14), channel_id=1, source_target_pairs={{0,25},{1,24},{2,26},{3,27},{4,28},{5,29},{6,31},{7,30},{8,16},{9,... | collective-permute-start | bytes 73736 | tf_op jit(solution)/shard_map/ppermute | solution.py:30
  15.3 0.0 collective-permute-start.6
  15.3 1.2 %collective-permute-start.5 = (f32[48,128]{1,0:T(8,128)S(1)}, f32[48,128]{1,0:T(8,128)S(1)}, u32[]{:S(2)}, u32[]{:S(2)}) collective-permute-start(f32[48,128]{1,0:T(8,128)S(1)} %get-tuple-element.16), channel_id=1, source_target_pairs={{0,9},{1,8},{2,10},{3,11},{4,13},{5,12},{6,14},{7,15},{8,1},{9,0},... | collective-permute-start | bytes 73736 | tf_op jit(solution)/shard_map/ppermute | solution.py:30
  16.5 1.0 %collective-permute-done.7.c_ref = f32[48,128]{1,0:T(8,128)S(1)} collective-permute-done((f32[48,128]{1,0:T(8,128)S(1)}, f32[48,128]{1,0:T(8,128)S(1)}, u32[]{:S(2)}, u32[]{:S(2)}) %collective-permute-start.7) | collective-permute-done | bytes 24608 | tf_op jit(solution)/shard_map/ppermute | solution.py:30
  17.5 2.2 %collective-permute-done.6.b_ref = f32[48,128]{1,0:T(8,128)S(1)} collective-permute-done((f32[48,128]{1,0:T(8,128)S(1)}, f32[48,128]{1,0:T(8,128)S(1)}, u32[]{:S(2)}, u32[]{:S(2)}) %collective-permute-start.6) | collective-permute-done | bytes 24608 | tf_op jit(solution)/shard_map/ppermute | solution.py:30
  19.7 0.0 collective-permute-done.5.a_ref
  19.7 0.8 %shard_map.40 = f32[48,96]{1,0:T(8,128)} custom-call(f32[48,128]{1,0:T(8,128)S(1)} %get-tuple-element.17.own_ref, f32[48,128]{1,0:T(8,128)S(1)} %collective-permute-done.5.a_ref, f32[48,128]{1,0:T(8,128)S(1)} %collective-permute-done.6.b_ref, f32[48,128]{1,0:T(8,128)S(1)} %collective-permute-done.7.c_ref), custom_call_target="tpu_custom_call" | custom-call | tf_op jit(solution)/shard_map/pallas_call | solution.py:154
  (5 shorter events, 0.1 us)
Async XLA Ops:
  2.4 2.8 %collective-permute-start.2 = (f32[2,48,384]{2,1,0:T(8,128)S(1)}, f32[2,48,384]{2,1,0:T(8,128)S(1)}, u32[]{:S(2)}, u32[]{:S(2)}) collective-permute-start(f32[2,48,384]{2,1,0:T(8,128)S(1)} %get-tuple-element.9), channel_id=1, source_target_pairs={{0,1},{1,0},{2,3},{3,2},{4,5},{5,4},{6,7},{7,6},{8,9},{9,8},{10,11... | collective-permute-start | bytes 442376 | tf_op jit(solution)/shard_map/ppermute | solution.py:30
  2.5 6.8 %collective-permute-start = (f32[2,48,384]{2,1,0:T(8,128)S(1)}, f32[2,48,384]{2,1,0:T(8,128)S(1)}, u32[]{:S(2)}, u32[]{:S(2)}) collective-permute-start(f32[2,48,384]{2,1,0:T(8,128)S(1)} %get-tuple-element.11), channel_id=1, source_target_pairs={{0,4},{1,5},{2,7},{3,6},{4,0},{5,1},{6,3},{7,2},{8,12},{9,13},{10,... | collective-permute-start | bytes 442376 | tf_op jit(solution)/shard_map/ppermute | solution.py:30
  5.2 4.9 %collective-permute-start.3 = (f32[48,384]{1,0:T(8,128)S(1)}, f32[48,384]{1,0:T(8,128)S(1)}, u32[]{:S(2)}, u32[]{:S(2)}) collective-permute-start(f32[48,384]{1,0:T(8,128)S(1)} %get-tuple-element.7), channel_id=1, source_target_pairs={{0,2},{1,3},{2,0},{3,1},{4,7},{5,6},{6,5},{7,4},{8,11},{9,10},{10,... | collective-permute-start | bytes 221192 | tf_op jit(solution)/shard_map/ppermute | solution.py:30
  6.5 5.7 %collective-permute-start.4 = (f32[48,384]{1,0:T(8,128)S(1)}, f32[48,384]{1,0:T(8,128)S(1)}, u32[]{:S(2)}, u32[]{:S(2)}) collective-permute-start(f32[48,384]{1,0:T(8,128)S(1)} %get-tuple-element.8), channel_id=1, source_target_pairs={{0,7},{1,6},{2,4},{3,5},{4,2},{5,3},{6,1},{7,0},{8,14},{9,15},{10,... | collective-permute-start | bytes 221192 | tf_op jit(solution)/shard_map/ppermute | solution.py:30
  9.4 2.8 %collective-permute-start.1 = (f32[48,384]{1,0:T(8,128)S(1)}, f32[48,384]{1,0:T(8,128)S(1)}, u32[]{:S(2)}, u32[]{:S(2)}) collective-permute-start(f32[48,384]{1,0:T(8,128)S(1)} %get-tuple-element.12), channel_id=1, source_target_pairs={{0,1},{1,0},{2,3},{3,2},{4,5},{5,4},{6,7},{7,6},{8,9},{9,8},{10,11... | collective-permute-start | bytes 221192 | tf_op jit(solution)/shard_map/ppermute | solution.py:30
  12.3 5.2 %collective-permute-start.7 = (f32[48,128]{1,0:T(8,128)S(1)}, f32[48,128]{1,0:T(8,128)S(1)}, u32[]{:S(2)}, u32[]{:S(2)}) collective-permute-start(f32[48,128]{1,0:T(8,128)S(1)} %get-tuple-element.14), channel_id=1, source_target_pairs={{0,25},{1,24},{2,26},{3,27},{4,28},{5,29},{6,31},{7,30},{8,16},{9,... | collective-permute-start | bytes 73736 | tf_op jit(solution)/shard_map/ppermute | solution.py:30
  15.3 4.4 %collective-permute-start.6 = (f32[48,128]{1,0:T(8,128)S(1)}, f32[48,128]{1,0:T(8,128)S(1)}, u32[]{:S(2)}, u32[]{:S(2)}) collective-permute-start(f32[48,128]{1,0:T(8,128)S(1)} %get-tuple-element.15), channel_id=1, source_target_pairs={{0,17},{1,16},{2,19},{3,18},{4,20},{5,21},{6,23},{7,22},{8,24},{9,... | collective-permute-start | bytes 73736 | tf_op jit(solution)/shard_map/ppermute | solution.py:30
  15.3 4.4 %collective-permute-start.5 = (f32[48,128]{1,0:T(8,128)S(1)}, f32[48,128]{1,0:T(8,128)S(1)}, u32[]{:S(2)}, u32[]{:S(2)}) collective-permute-start(f32[48,128]{1,0:T(8,128)S(1)} %get-tuple-element.16), channel_id=1, source_target_pairs={{0,9},{1,8},{2,10},{3,11},{4,13},{5,12},{6,14},{7,15},{8,1},{9,0},... | collective-permute-start | bytes 73736 | tf_op jit(solution)/shard_map/ppermute | solution.py:30

commit v5 on v4

--- a/solution.py
+++ b/solution.py
@@ -8,7 +8,7 @@
 from jax.sharding import PartitionSpec as P
 
 BOTH = ("aux", "occ")
-FLIPS = (((0, 1, 1, 1), (0, 1, 0, 0)), ((0, 0, 1, 0), (1, 1, 0, 0)))
+FLIPS = (((0, 1, 1, 1), (0, 1, 0, 0)), ((0, 0, 1, 0), (1, 1, 1, 0)))
 FLIP_BITS = sum(FLIPS[x][y][z] << (x * 8 + y * 4 + z) for x in range(2) for y in range(2) for z in range(4))
 PLANE = ((1, 0, 0), (1, 1, 0))
 LINE = ((0, 0, 1), (0, 0, 2), (0, 0, 3))
@@ -41,19 +41,22 @@
     blk = nbasis // nblocks
     rows, cols = nbasis // 8, nbasis // 4
 
-    copies = (
-        pltpu.make_async_copy(ground_hbm, ground, sems.at[0]),
-        pltpu.make_async_copy(response_hbm, response, sems.at[1]),
-        pltpu.make_async_copy(pattern_hbm, pattern, sems.at[2]),
-    )
-    for copy in copies:
-        copy.start()
+    step = ground.shape[0] // 1
+    parts = [pl.ds(k * step, step) for k in range(1)]
+    firsts = [pltpu.make_async_copy(ground_hbm.at[here], ground.at[here], sems.at[3 + k]) for k, here in enumerate(parts)]
+    second = pltpu.make_async_copy(response_hbm, response, sems.at[0])
+    masks = pltpu.make_async_copy(pattern_hbm, pattern, sems.at[1])
+    for first in firsts:
+        first.start()
+    second.start()
+    masks.start()
     x, y, z, core = place()
     kind = core ^ (FLIP_BITS >> (x * 8 + y * 4 + z)) & 1
-    copies[0].wait()
-    turned[...] = ground[...].T
-    copies[1].wait()
-    copies[2].wait()
+    for first, here in zip(firsts, parts):
+        first.wait()
+        turned[:, here] = ground[here, :].T
+    second.wait()
+    masks.wait()
     block = lax.dot_general(turned[0:128, :], response[...], (((1,), (0,)), ((), ())), preferred_element_type=jnp.float32)
     for j in range(3):
         product[0:128, 128 * j : 128 * j + 128] = 0.5 * pattern[0, j].astype(jnp.float32) * block[:, 128 * j : 128 * j + 128]
@@ -71,10 +74,10 @@
     lane = lax.broadcasted_iota(jnp.int32, (rows, nbasis), 1)
     even = sum(((lane >= rows * k).astype(jnp.int32) for k in range(1, 8))) & 1 == 0
     z_to = sum((lane >= cols * k).astype(jnp.int32) for k in range(1, 4))
-    for turn in range(2):
-        x_to = x ^ turn
-        base = pl.multiple_of(2 * cols * x_to, 8)
-        upper, lower = ([whole[pl.ds(base + cols * c + at, rows), :] for c in range(2)] for at in (0, rows))
+    for x_to in range(2):
+        turn = x ^ x_to
+        base = 2 * cols * x_to
+        upper, lower = ([whole[base + cols * c + at : base + cols * c + at + rows, :] for c in range(2)] for at in (0, rows))
         for y_to in range(2):
             if y_to == 0:
                 tiles = [jnp.where(even, u, pltpu.roll(d, rows, 1)) for u, d in zip(upper, lower)]
@@ -82,9 +85,9 @@
                 tiles = [jnp.where(even, pltpu.roll(u, nbasis - rows, 1), d) for u, d in zip(upper, lower)]
             flips = lax.shift_right_logical(jnp.full_like(z_to, FLIP_BITS), x_to * 8 + y_to * 4 + z_to) & 1
             other = (flips ^ kind) == 0
-            stay, away = ((0, 6), (1, 6)) if turn == 0 else ((2, 1), (4, 1))
-            out_ref[stay[0] + stay[1] * (y ^ y_to), :, :] = jnp.where(other, tiles[0], tiles[1])
-            out_ref[away[0] + away[1] * (y ^ y_to), :, :] = jnp.where(other, tiles[1], tiles[0])
+            step = y ^ y_to
+            out_ref[turn * (2 + step) + (1 - turn) * 6 * step, :, :] = jnp.where(other, tiles[0], tiles[1])
+            out_ref[turn * (4 + step) + (1 - turn) * (1 + 6 * step), :, :] = jnp.where(other, tiles[1], tiles[0])
 
 
 def side_kernel(own_ref, came_ref, x_ref, y_ref):
@@ -126,7 +129,7 @@
             pltpu.VMEM((nbasis, nbasis), jnp.float32),
             pltpu.VMEM((nbasis, nbasis), jnp.float32),
             pltpu.VMEM((nbasis, depth), jnp.bfloat16),
-            pltpu.SemaphoreType.DMA((3,)),
+            pltpu.SemaphoreType.DMA((4,)),
         ],
         compiler_params=params,
     )(*(pltpu.with_memory_space_constraint(a, pltpu.HBM) for a in inputs))

time: 20.6 us -> 20.6 us (level)
  no operation moved by 1% of the time
where the time goes in v5:
time: 20.6 us; the launch traced here: 20.3 us
  starting transfers between devices  10.2 us (50%)
  waiting for transfers between devices  6.77 us (33%)
  Pallas kernels  3.18 us (15%)
    ppermute x8, starting transfers between devices, swap(): return lax.ppermute(value, BOTH, pairs(move))  10.2 us
    ppermute x8, waiting for transfers between devices, swap(): return lax.ppermute(value, BOTH, pairs(move))  6.77 us
    pallas_call x1, Pallas kernels, fast_shards(): pl.pallas_call(product_kernel, out_shape=jax.ShapeDtypeStruct((8, rows, n...  2.3 us
    pallas_call x1, Pallas kernels, fast_shards(): pl.pallas_call(turn_kernel, out_shape=jax.ShapeDtypeStruct((rows, cols),...  0.77 us
  transfers between devices with their start and end apart: 8, of which 4 were waited for; matrix products, arithmetic and copies ran while one was open for 0% of the time, Pallas kernels for 0%

profile of v5, /device:TPU:1, one launch (start us, length us, event | category | flops | bytes accessed | tf_op | source)
XLA Modules:
  0.0 20.3 jit_solution(18162562153189767465)
XLA Ops:
  0.0 2.3 %shard_map.37 = f32[8,48,384]{2,1,0:T(8,128)S(1)} custom-call(s32[3,3]{1,0:T(4,128)} %pattern_hbm.1, bf16[1024,384]{1,0:T(8,128)(2,1)} %bitcast.14, bf16[1024,384]{1,0:T(8,128)(2,1)} %bitcast.15), custom_call_target="tpu_custom_call" | custom-call | tf_op jit(solution)/shard_map/pallas_call | solution.py:120
  2.3 0.1 collective-permute-start.2
  2.5 2.7 %collective-permute-start = (f32[2,48,384]{2,1,0:T(8,128)S(1)}, f32[2,48,384]{2,1,0:T(8,128)S(1)}, u32[]{:S(2)}, u32[]{:S(2)}) collective-permute-start(f32[2,48,384]{2,1,0:T(8,128)S(1)} %get-tuple-element.11), channel_id=1, source_target_pairs={{0,4},{1,5},{2,7},{3,6},{4,0},{5,1},{6,3},{7,2},{8,12},{9,13},{10,... | collective-permute-start | bytes 442376 | tf_op jit(solution)/shard_map/ppermute | solution.py:30
  5.2 0.0 collective-permute-done.2.came_ref
  5.2 1.2 %collective-permute-start.3 = (f32[48,384]{1,0:T(8,128)S(1)}, f32[48,384]{1,0:T(8,128)S(1)}, u32[]{:S(2)}, u32[]{:S(2)}) collective-permute-start(f32[48,384]{1,0:T(8,128)S(1)} %get-tuple-element.7), channel_id=1, source_target_pairs={{0,2},{1,3},{2,0},{3,1},{4,7},{5,6},{6,5},{7,4},{8,11},{9,10},{10,... | collective-permute-start | bytes 221192 | tf_op jit(solution)/shard_map/ppermute | solution.py:30
  6.4 1.3 %collective-permute-start.4 = (f32[48,384]{1,0:T(8,128)S(1)}, f32[48,384]{1,0:T(8,128)S(1)}, u32[]{:S(2)}, u32[]{:S(2)}) collective-permute-start(f32[48,384]{1,0:T(8,128)S(1)} %get-tuple-element.8), channel_id=1, source_target_pairs={{0,7},{1,6},{2,4},{3,5},{4,2},{5,3},{6,1},{7,0},{8,14},{9,15},{10,... | collective-permute-start | bytes 221192 | tf_op jit(solution)/shard_map/ppermute | solution.py:30
  7.7 1.6 %collective-permute-done = f32[2,48,384]{2,1,0:T(8,128)S(1)} collective-permute-done((f32[2,48,384]{2,1,0:T(8,128)S(1)}, f32[2,48,384]{2,1,0:T(8,128)S(1)}, u32[]{:S(2)}, u32[]{:S(2)}) %collective-permute-start) | collective-permute-done | bytes 147488 | tf_op jit(solution)/shard_map/ppermute | solution.py:30
  9.3 0.7 %collective-permute-start.1 = (f32[48,384]{1,0:T(8,128)S(1)}, f32[48,384]{1,0:T(8,128)S(1)}, u32[]{:S(2)}, u32[]{:S(2)}) collective-permute-start(f32[48,384]{1,0:T(8,128)S(1)} %get-tuple-element.12), channel_id=1, source_target_pairs={{0,1},{1,0},{2,3},{3,2},{4,5},{5,4},{6,7},{7,6},{8,9},{9,8},{10,11... | collective-permute-start | bytes 221192 | tf_op jit(solution)/shard_map/ppermute | solution.py:30
  10.1 0.0 collective-permute-done.3.b_ref
  10.1 2.1 %collective-permute-done.4.c_ref = f32[48,384]{1,0:T(8,128)S(1)} collective-permute-done((f32[48,384]{1,0:T(8,128)S(1)}, f32[48,384]{1,0:T(8,128)S(1)}, u32[]{:S(2)}, u32[]{:S(2)}) %collective-permute-start.4) | collective-permute-done | bytes 73760 | tf_op jit(solution)/shard_map/ppermute | solution.py:30
  12.1 0.0 collective-permute-done.1.a_ref
  12.1 0.1 shard_map.39
  12.3 3.0 %collective-permute-start.7 = (f32[48,128]{1,0:T(8,128)S(1)}, f32[48,128]{1,0:T(8,128)S(1)}, u32[]{:S(2)}, u32[]{:S(2)}) collective-permute-start(f32[48,128]{1,0:T(8,128)S(1)} %get-tuple-element.14), channel_id=1, source_target_pairs={{0,25},{1,24},{2,26},{3,27},{4,28},{5,29},{6,31},{7,30},{8,16},{9,... | collective-permute-start | bytes 73736 | tf_op jit(solution)/shard_map/ppermute | solution.py:30
  15.3 0.0 collective-permute-start.6
  15.3 1.2 %collective-permute-start.5 = (f32[48,128]{1,0:T(8,128)S(1)}, f32[48,128]{1,0:T(8,128)S(1)}, u32[]{:S(2)}, u32[]{:S(2)}) collective-permute-start(f32[48,128]{1,0:T(8,128)S(1)} %get-tuple-element.16), channel_id=1, source_target_pairs={{0,9},{1,8},{2,10},{3,11},{4,13},{5,12},{6,14},{7,15},{8,1},{9,0},... | collective-permute-start | bytes 73736 | tf_op jit(solution)/shard_map/ppermute | solution.py:30
  16.4 1.2 %collective-permute-done.7.c_ref = f32[48,128]{1,0:T(8,128)S(1)} collective-permute-done((f32[48,128]{1,0:T(8,128)S(1)}, f32[48,128]{1,0:T(8,128)S(1)}, u32[]{:S(2)}, u32[]{:S(2)}) %collective-permute-start.7) | collective-permute-done | bytes 24608 | tf_op jit(solution)/shard_map/ppermute | solution.py:30
  17.6 1.9 %collective-permute-done.6.b_ref = f32[48,128]{1,0:T(8,128)S(1)} collective-permute-done((f32[48,128]{1,0:T(8,128)S(1)}, f32[48,128]{1,0:T(8,128)S(1)}, u32[]{:S(2)}, u32[]{:S(2)}) %collective-permute-start.6) | collective-permute-done | bytes 24608 | tf_op jit(solution)/shard_map/ppermute | solution.py:30
  19.6 0.0 collective-permute-done.5.a_ref
  19.6 0.8 %shard_map.40 = f32[48,96]{1,0:T(8,128)} custom-call(f32[48,128]{1,0:T(8,128)S(1)} %get-tuple-element.17.own_ref, f32[48,128]{1,0:T(8,128)S(1)} %collective-permute-done.5.a_ref, f32[48,128]{1,0:T(8,128)S(1)} %collective-permute-done.6.b_ref, f32[48,128]{1,0:T(8,128)S(1)} %collective-permute-done.7.c_ref), custom_call_target="tpu_custom_call" | custom-call | tf_op jit(solution)/shard_map/pallas_call | solution.py:157
  (5 shorter events, 0.1 us)
Async XLA Ops:
  2.3 2.8 %collective-permute-start.2 = (f32[2,48,384]{2,1,0:T(8,128)S(1)}, f32[2,48,384]{2,1,0:T(8,128)S(1)}, u32[]{:S(2)}, u32[]{:S(2)}) collective-permute-start(f32[2,48,384]{2,1,0:T(8,128)S(1)} %get-tuple-element.9), channel_id=1, source_target_pairs={{0,1},{1,0},{2,3},{3,2},{4,5},{5,4},{6,7},{7,6},{8,9},{9,8},{10,11... | collective-permute-start | bytes 442376 | tf_op jit(solution)/shard_map/ppermute | solution.py:30
  2.5 6.8 %collective-permute-start = (f32[2,48,384]{2,1,0:T(8,128)S(1)}, f32[2,48,384]{2,1,0:T(8,128)S(1)}, u32[]{:S(2)}, u32[]{:S(2)}) collective-permute-start(f32[2,48,384]{2,1,0:T(8,128)S(1)} %get-tuple-element.11), channel_id=1, source_target_pairs={{0,4},{1,5},{2,7},{3,6},{4,0},{5,1},{6,3},{7,2},{8,12},{9,13},{10,... | collective-permute-start | bytes 442376 | tf_op jit(solution)/shard_map/ppermute | solution.py:30
  5.2 4.9 %collective-permute-start.3 = (f32[48,384]{1,0:T(8,128)S(1)}, f32[48,384]{1,0:T(8,128)S(1)}, u32[]{:S(2)}, u32[]{:S(2)}) collective-permute-start(f32[48,384]{1,0:T(8,128)S(1)} %get-tuple-element.7), channel_id=1, source_target_pairs={{0,2},{1,3},{2,0},{3,1},{4,7},{5,6},{6,5},{7,4},{8,11},{9,10},{10,... | collective-permute-start | bytes 221192 | tf_op jit(solution)/shard_map/ppermute | solution.py:30
  6.4 5.7 %collective-permute-start.4 = (f32[48,384]{1,0:T(8,128)S(1)}, f32[48,384]{1,0:T(8,128)S(1)}, u32[]{:S(2)}, u32[]{:S(2)}) collective-permute-start(f32[48,384]{1,0:T(8,128)S(1)} %get-tuple-element.8), channel_id=1, source_target_pairs={{0,7},{1,6},{2,4},{3,5},{4,2},{5,3},{6,1},{7,0},{8,14},{9,15},{10,... | collective-permute-start | bytes 221192 | tf_op jit(solution)/shard_map/ppermute | solution.py:30
  9.3 2.8 %collective-permute-start.1 = (f32[48,384]{1,0:T(8,128)S(1)}, f32[48,384]{1,0:T(8,128)S(1)}, u32[]{:S(2)}, u32[]{:S(2)}) collective-permute-start(f32[48,384]{1,0:T(8,128)S(1)} %get-tuple-element.12), channel_id=1, source_target_pairs={{0,1},{1,0},{2,3},{3,2},{4,5},{5,4},{6,7},{7,6},{8,9},{9,8},{10,11... | collective-permute-start | bytes 221192 | tf_op jit(solution)/shard_map/ppermute | solution.py:30
  12.3 5.3 %collective-permute-start.7 = (f32[48,128]{1,0:T(8,128)S(1)}, f32[48,128]{1,0:T(8,128)S(1)}, u32[]{:S(2)}, u32[]{:S(2)}) collective-permute-start(f32[48,128]{1,0:T(8,128)S(1)} %get-tuple-element.14), channel_id=1, source_target_pairs={{0,25},{1,24},{2,26},{3,27},{4,28},{5,29},{6,31},{7,30},{8,16},{9,... | collective-permute-start | bytes 73736 | tf_op jit(solution)/shard_map/ppermute | solution.py:30
  15.3 4.3 %collective-permute-start.6 = (f32[48,128]{1,0:T(8,128)S(1)}, f32[48,128]{1,0:T(8,128)S(1)}, u32[]{:S(2)}, u32[]{:S(2)}) collective-permute-start(f32[48,128]{1,0:T(8,128)S(1)} %get-tuple-element.15), channel_id=1, source_target_pairs={{0,17},{1,16},{2,19},{3,18},{4,20},{5,21},{6,22},{7,23},{8,24},{9,... | collective-permute-start | bytes 73736 | tf_op jit(solution)/shard_map/ppermute | solution.py:30
  15.3 4.3 %collective-permute-start.5 = (f32[48,128]{1,0:T(8,128)S(1)}, f32[48,128]{1,0:T(8,128)S(1)}, u32[]{:S(2)}, u32[]{:S(2)}) collective-permute-start(f32[48,128]{1,0:T(8,128)S(1)} %get-tuple-element.16), channel_id=1, source_target_pairs={{0,9},{1,8},{2,10},{3,11},{4,13},{5,12},{6,14},{7,15},{8,1},{9,0},... | collective-permute-start | bytes 73736 | tf_op jit(solution)/shard_map/ppermute | solution.py:30

commit v6 on v5

--- a/solution.py
+++ b/solution.py
@@ -1,5 +1,3 @@
-import functools
-
 import jax
 import jax.numpy as jnp
 from jax import lax
@@ -8,26 +6,29 @@
 from jax.sharding import PartitionSpec as P
 
 BOTH = ("aux", "occ")
-FLIPS = (((0, 1, 1, 1), (0, 1, 0, 0)), ((0, 0, 1, 0), (1, 1, 1, 0)))
+FLIPS = (((1, 1, 0, 1), (0, 1, 1, 1)), ((0, 0, 1, 0), (0, 0, 0, 1)))
 FLIP_BITS = sum(FLIPS[x][y][z] << (x * 8 + y * 4 + z) for x in range(2) for y in range(2) for z in range(4))
 PLANE = ((1, 0, 0), (1, 1, 0))
-LINE = ((0, 0, 1), (0, 0, 2), (0, 0, 3))
-
-
-def pairs(move):
-    if move is None:
+FIRST = (0, 1, 0)
+NEAR = (0, 0, 1)
+FAR = ((0, 0, 3), (0, 0, 2))
+
+
+def pairs(moves):
+    if not moves:
         return [(i, i ^ 1) for i in range(32)]
     found = []
     for i in range(32):
         x, y, z, core = i >> 1 & 1, i >> 2 & 1, i >> 3, i & 1
         kind = core ^ FLIPS[x][y][z]
+        move = moves[kind]
         x, y, z = x ^ move[0], y ^ move[1], z ^ move[2]
         found.append((i, ((z * 2 + y) * 2 + x) * 2 + (kind ^ FLIPS[x][y][z])))
     return found
 
 
-def swap(value, move):
-    return lax.ppermute(value, BOTH, pairs(move))
+def swap(value, *moves):
+    return lax.ppermute(value, BOTH, pairs(moves))
 
 
 def place():
@@ -71,23 +72,32 @@
             at_i, at_j = slice(i * blk, (i + 1) * blk), slice(j * blk, (j + 1) * blk)
             whole[at_i, at_j] = product[at_i, at_j] + product[at_j, at_i].T
 
-    lane = lax.broadcasted_iota(jnp.int32, (rows, nbasis), 1)
-    even = sum(((lane >= rows * k).astype(jnp.int32) for k in range(1, 8))) & 1 == 0
+    lane = lax.broadcasted_iota(jnp.int32, (8, nbasis), 1)
+    even = sum((lane >= rows * k).astype(jnp.int32) for k in range(1, 8)) & 1 == 0
     z_to = sum((lane >= cols * k).astype(jnp.int32) for k in range(1, 4))
+    left, two, three = z_to & 1 == 0, z_to == z ^ 2, z_to == z ^ 3
+    mine = jnp.full_like(lane, kind) == 0
+
+    def cut(at):
+        return whole[at : at + rows, :].reshape(rows // 8, 8, nbasis)
+
     for x_to in range(2):
         turn = x ^ x_to
-        base = 2 * cols * x_to
-        upper, lower = ([whole[base + cols * c + at : base + cols * c + at + rows, :] for c in range(2)] for at in (0, rows))
+        upper, lower = ([cut(cols * (2 * x_to + c) + at) for c in range(2)] for at in (0, rows))
         for y_to in range(2):
             if y_to == 0:
-                tiles = [jnp.where(even, u, pltpu.roll(d, rows, 1)) for u, d in zip(upper, lower)]
+                tiles = [jnp.where(even, u, pltpu.roll(d, rows, 2)) for u, d in zip(upper, lower)]
             else:
-                tiles = [jnp.where(even, pltpu.roll(u, nbasis - rows, 1), d) for u, d in zip(upper, lower)]
-            flips = lax.shift_right_logical(jnp.full_like(z_to, FLIP_BITS), x_to * 8 + y_to * 4 + z_to) & 1
-            other = (flips ^ kind) == 0
+                tiles = [jnp.where(even, pltpu.roll(u, nbasis - rows, 2), d) for u, d in zip(upper, lower)]
+            flips = lax.shift_right_logical(jnp.full_like(z_to, FLIP_BITS), x_to * 8 + y_to * 4 + z_to) & 1 == 0
+            zero, one = jnp.where(flips, tiles[0], tiles[1]), jnp.where(flips, tiles[1], tiles[0])
+            moved = jnp.where(three, one, zero)
+            moved = jnp.where(left, pltpu.roll(moved, nbasis - cols, 2), pltpu.roll(moved, cols, 2))
+            zero, one = jnp.where(two, moved, zero), jnp.where(three, moved, one)
             step = y ^ y_to
-            out_ref[turn * (2 + step) + (1 - turn) * 6 * step, :, :] = jnp.where(other, tiles[0], tiles[1])
-            out_ref[turn * (4 + step) + (1 - turn) * (1 + 6 * step), :, :] = jnp.where(other, tiles[1], tiles[0])
+            own, other = jnp.where(mine, zero, one), jnp.where(mine, one, zero)
+            out_ref[turn * (2 + step) + (1 - turn) * 6 * step, :, :] = own.reshape(rows, nbasis)
+            out_ref[turn * (4 + step) + (1 - turn) * (1 + 6 * step), :, :] = other.reshape(rows, nbasis)
 
 
 def side_kernel(own_ref, came_ref, x_ref, y_ref):
@@ -99,8 +109,11 @@
     cols = own_ref.shape[1] // 4
     total = own_ref[...] + a_ref[...] + b_ref[...] + c_ref[...]
     x, y, z, core = place()
+    kind = core ^ (FLIP_BITS >> (x * 8 + y * 4 + z)) & 1
     for z_to in range(4):
-        out_ref[z ^ z_to, :, :cols] = total[:, cols * z_to : cols * (z_to + 1)]
+        turn = z ^ z_to
+        slot = jnp.where((turn >= 2) & (kind == 0), 5 - turn, turn)
+        out_ref[slot, :, :cols] = total[:, cols * z_to : cols * (z_to + 1)]
 
 
 def turn_kernel(own_ref, a_ref, b_ref, c_ref, out_ref):
@@ -141,11 +154,11 @@
         out_specs=(vmem, vmem),
         cost_estimate=pl.CostEstimate(flops=100000, bytes_accessed=600000, transcendentals=0),
         compiler_params=params,
-    )(parts[2:4], swap(parts[4:6], None))
-    far = swap(parts[6:8], (0, 1, 0))
-    near = [swap(sides[move[1]], move) for move in PLANE]
-    own = parts[0:2] + far
-    plane = [swap(own[1], None), *near]
+    )(parts[2:4], swap(parts[4:6]))
+    first = swap(parts[6:8], FIRST, FIRST)
+    near = [swap(sides[move[1]], move, move) for move in PLANE]
+    own = parts[0:2] + first
+    plane = [swap(own[1]), *near]
     line = pl.pallas_call(
         split_kernel,
         out_shape=jax.ShapeDtypeStruct((4, rows, 128), jnp.float32),
@@ -153,7 +166,8 @@
         out_specs=vmem,
         compiler_params=params,
     )(own[0], *plane)
-    last = [swap(line[move[2]], move) for move in LINE]
+    far = swap(line[2:], *FAR)
+    last = [swap(line[1], NEAR, NEAR), swap(far[1]), far[0]]
     return pl.pallas_call(
         turn_kernel,
         out_shape=jax.ShapeDtypeStruct((rows, cols), jnp.float32),

time: 20.6 us -> 19.8 us (0.961)
  the two profiles are of different devices: /device:TPU:1 before, /device:TPU:7 now
where the time goes in v6:
time: 19.8 us; the launch traced here: 19.6 us
  starting transfers between devices  8.39 us (42%)
  waiting for transfers between devices  7.74 us (39%)
  Pallas kernels  3.38 us (17%)
    ppermute x8, starting transfers between devices, swap(): return lax.ppermute(value, BOTH, pairs(moves))  8.39 us
    ppermute x8, waiting for transfers between devices, swap(): return lax.ppermute(value, BOTH, pairs(moves))  7.74 us
    pallas_call x1, Pallas kernels, fast_shards(): pl.pallas_call(product_kernel, out_shape=jax.ShapeDtypeStruct((8, rows, n...  2.49 us
    pallas_call x1, Pallas kernels, fast_shards(): pl.pallas_call(turn_kernel, out_shape=jax.ShapeDtypeStruct((rows, cols),...  0.77 us
  transfers between devices with their start and end apart: 8, of which 5 were waited for; matrix products, arithmetic and copies ran while one was open for 0% of the time, Pallas kernels for 0%

profile of v6, /device:TPU:7, one launch (start us, length us, event | category | flops | bytes accessed | tf_op | source)
XLA Modules:
  0.0 19.6 jit_solution(5536736179169236241)
XLA Ops:
  0.0 2.5 %shard_map.37 = f32[8,48,384]{2,1,0:T(8,128)S(1)} custom-call(s32[3,3]{1,0:T(4,128)} %pattern_hbm.1, bf16[1024,384]{1,0:T(8,128)(2,1)} %bitcast.14, bf16[1024,384]{1,0:T(8,128)(2,1)} %bitcast.15), custom_call_target="tpu_custom_call" | custom-call | tf_op jit(solution)/shard_map/pallas_call | solution.py:133
  2.5 0.7 %collective-permute-start.2 = (f32[2,48,384]{2,1,0:T(8,128)S(1)}, f32[2,48,384]{2,1,0:T(8,128)S(1)}, u32[]{:S(2)}, u32[]{:S(2)}) collective-permute-start(f32[2,48,384]{2,1,0:T(8,128)S(1)} %get-tuple-element.9), channel_id=1, source_target_pairs={{0,1},{1,0},{2,3},{3,2},{4,5},{5,4},{6,7},{7,6},{8,9},{9,8},{10,11... | collective-permute-start | bytes 442376 | tf_op jit(solution)/shard_map/ppermute | solution.py:31
  3.3 0.2 %collective-permute-start = (f32[2,48,384]{2,1,0:T(8,128)S(1)}, f32[2,48,384]{2,1,0:T(8,128)S(1)}, u32[]{:S(2)}, u32[]{:S(2)}) collective-permute-start(f32[2,48,384]{2,1,0:T(8,128)S(1)} %get-tuple-element.11), channel_id=1, source_target_pairs={{0,5},{1,4},{2,6},{3,7},{4,1},{5,0},{6,2},{7,3},{8,12},{9,13},{10,... | collective-permute-start | bytes 442376 | tf_op jit(solution)/shard_map/ppermute | solution.py:31
  3.5 0.8 %collective-permute-done.2.came_ref = f32[2,48,384]{2,1,0:T(8,128)S(1)} collective-permute-done((f32[2,48,384]{2,1,0:T(8,128)S(1)}, f32[2,48,384]{2,1,0:T(8,128)S(1)}, u32[]{:S(2)}, u32[]{:S(2)}) %collective-permute-start.2) | collective-permute-done | bytes 147488 | tf_op jit(solution)/shard_map/ppermute | solution.py:31
  4.3 0.3 %collective-permute-start.3 = (f32[48,384]{1,0:T(8,128)S(1)}, f32[48,384]{1,0:T(8,128)S(1)}, u32[]{:S(2)}, u32[]{:S(2)}) collective-permute-start(f32[48,384]{1,0:T(8,128)S(1)} %get-tuple-element.7), channel_id=1, source_target_pairs={{0,3},{1,2},{2,1},{3,0},{4,6},{5,7},{6,4},{7,5},{8,11},{9,10},{10,... | collective-permute-start | bytes 221192 | tf_op jit(solution)/shard_map/ppermute | solution.py:31
  4.6 1.7 %collective-permute-start.4 = (f32[48,384]{1,0:T(8,128)S(1)}, f32[48,384]{1,0:T(8,128)S(1)}, u32[]{:S(2)}, u32[]{:S(2)}) collective-permute-start(f32[48,384]{1,0:T(8,128)S(1)} %get-tuple-element.8), channel_id=1, source_target_pairs={{0,7},{1,6},{2,4},{3,5},{4,2},{5,3},{6,1},{7,0},{8,15},{9,14},{10,... | collective-permute-start | bytes 221192 | tf_op jit(solution)/shard_map/ppermute | solution.py:31
  6.3 2.4 %collective-permute-done = f32[2,48,384]{2,1,0:T(8,128)S(1)} collective-permute-done((f32[2,48,384]{2,1,0:T(8,128)S(1)}, f32[2,48,384]{2,1,0:T(8,128)S(1)}, u32[]{:S(2)}, u32[]{:S(2)}) %collective-permute-start) | collective-permute-done | bytes 147488 | tf_op jit(solution)/shard_map/ppermute | solution.py:31
  8.7 2.5 %collective-permute-start.1 = (f32[48,384]{1,0:T(8,128)S(1)}, f32[48,384]{1,0:T(8,128)S(1)}, u32[]{:S(2)}, u32[]{:S(2)}) collective-permute-start(f32[48,384]{1,0:T(8,128)S(1)} %get-tuple-element.12), channel_id=1, source_target_pairs={{0,1},{1,0},{2,3},{3,2},{4,5},{5,4},{6,7},{7,6},{8,9},{9,8},{10,11... | collective-permute-start | bytes 221192 | tf_op jit(solution)/shard_map/ppermute | solution.py:31
  11.2 0.0 collective-permute-done.3.b_ref
  11.2 0.0 collective-permute-done.4.c_ref
  11.2 0.9 %collective-permute-done.1.a_ref = f32[48,384]{1,0:T(8,128)S(1)} collective-permute-done((f32[48,384]{1,0:T(8,128)S(1)}, f32[48,384]{1,0:T(8,128)S(1)}, u32[]{:S(2)}, u32[]{:S(2)}) %collective-permute-start.1) | collective-permute-done | bytes 73760 | tf_op jit(solution)/shard_map/ppermute | solution.py:31
  12.2 0.1 shard_map.39
  12.3 0.7 %collective-permute-start.6 = (f32[2,48,128]{2,1,0:T(8,128)S(1)}, f32[2,48,128]{2,1,0:T(8,128)S(1)}, u32[]{:S(2)}, u32[]{:S(2)}) collective-permute-start(f32[2,48,128]{2,1,0:T(8,128)S(1)} %slice.52), channel_id=1, source_target_pairs={{0,17},{1,25},{2,26},{3,18},{4,29},{5,20},{6,31},{7,23},{8,24},{9,... | collective-permute-start | bytes 147464 | tf_op jit(solution)/shard_map/ppermute | solution.py:31
  13.0 1.8 %collective-permute-start.5 = (f32[48,128]{1,0:T(8,128)S(1)}, f32[48,128]{1,0:T(8,128)S(1)}, u32[]{:S(2)}, u32[]{:S(2)}) collective-permute-start(f32[48,128]{1,0:T(8,128)S(1)} %get-tuple-element.14), channel_id=1, source_target_pairs={{0,8},{1,9},{2,10},{3,11},{4,13},{5,12},{6,14},{7,15},{8,0},{9,1},... | collective-permute-start | bytes 73736 | tf_op jit(solution)/shard_map/ppermute | solution.py:31
  14.8 2.8 %collective-permute-done.6 = f32[2,48,128]{2,1,0:T(8,128)S(1)} collective-permute-done((f32[2,48,128]{2,1,0:T(8,128)S(1)}, f32[2,48,128]{2,1,0:T(8,128)S(1)}, u32[]{:S(2)}, u32[]{:S(2)}) %collective-permute-start.6) | collective-permute-done | bytes 49184 | tf_op jit(solution)/shard_map/ppermute | solution.py:31
  17.6 0.4 %collective-permute-start.7 = (f32[48,128]{1,0:T(8,128)S(1)}, f32[48,128]{1,0:T(8,128)S(1)}, u32[]{:S(2)}, u32[]{:S(2)}) collective-permute-start(f32[48,128]{1,0:T(8,128)S(1)} %get-tuple-element.17), channel_id=1, source_target_pairs={{0,1},{1,0},{2,3},{3,2},{4,5},{5,4},{6,7},{7,6},{8,9},{9,8},{10,11... | collective-permute-start | bytes 73736 | tf_op jit(solution)/shard_map/ppermute | solution.py:31
  18.0 0.0 collective-permute-done.5.a_ref
  18.0 0.8 %collective-permute-done.7.b_ref = f32[48,128]{1,0:T(8,128)S(1)} collective-permute-done((f32[48,128]{1,0:T(8,128)S(1)}, f32[48,128]{1,0:T(8,128)S(1)}, u32[]{:S(2)}, u32[]{:S(2)}) %collective-permute-start.7) | collective-permute-done | bytes 24608 | tf_op jit(solution)/shard_map/ppermute | solution.py:31
  18.9 0.8 %shard_map.40 = f32[48,96]{1,0:T(8,128)} custom-call(f32[48,128]{1,0:T(8,128)S(1)} %get-tuple-element.15.own_ref, f32[48,128]{1,0:T(8,128)S(1)} %collective-permute-done.5.a_ref, f32[48,128]{1,0:T(8,128)S(1)} %collective-permute-done.7.b_ref, f32[48,128]{1,0:T(8,128)S(1)} %get-tuple-element.16.c_ref), custom_call_target="tpu_custom_call" | custom-call | tf_op jit(solution)/shard_map/pallas_call | solution.py:171
  (7 shorter events, 0.1 us)
Async XLA Ops:
  2.5 1.7 %collective-permute-start.2 = (f32[2,48,384]{2,1,0:T(8,128)S(1)}, f32[2,48,384]{2,1,0:T(8,128)S(1)}, u32[]{:S(2)}, u32[]{:S(2)}) collective-permute-start(f32[2,48,384]{2,1,0:T(8,128)S(1)} %get-tuple-element.9), channel_id=1, source_target_pairs={{0,1},{1,0},{2,3},{3,2},{4,5},{5,4},{6,7},{7,6},{8,9},{9,8},{10,11... | collective-permute-start | bytes 442376 | tf_op jit(solution)/shard_map/ppermute | solution.py:31
  3.3 5.4 %collective-permute-start = (f32[2,48,384]{2,1,0:T(8,128)S(1)}, f32[2,48,384]{2,1,0:T(8,128)S(1)}, u32[]{:S(2)}, u32[]{:S(2)}) collective-permute-start(f32[2,48,384]{2,1,0:T(8,128)S(1)} %get-tuple-element.11), channel_id=1, source_target_pairs={{0,5},{1,4},{2,6},{3,7},{4,1},{5,0},{6,2},{7,3},{8,12},{9,13},{10,... | collective-permute-start | bytes 442376 | tf_op jit(solution)/shard_map/ppermute | solution.py:31
  4.3 6.9 %collective-permute-start.3 = (f32[48,384]{1,0:T(8,128)S(1)}, f32[48,384]{1,0:T(8,128)S(1)}, u32[]{:S(2)}, u32[]{:S(2)}) collective-permute-start(f32[48,384]{1,0:T(8,128)S(1)} %get-tuple-element.7), channel_id=1, source_target_pairs={{0,3},{1,2},{2,1},{3,0},{4,6},{5,7},{6,4},{7,5},{8,11},{9,10},{10,... | collective-permute-start | bytes 221192 | tf_op jit(solution)/shard_map/ppermute | solution.py:31
  4.6 6.6 %collective-permute-start.4 = (f32[48,384]{1,0:T(8,128)S(1)}, f32[48,384]{1,0:T(8,128)S(1)}, u32[]{:S(2)}, u32[]{:S(2)}) collective-permute-start(f32[48,384]{1,0:T(8,128)S(1)} %get-tuple-element.8), channel_id=1, source_target_pairs={{0,7},{1,6},{2,4},{3,5},{4,2},{5,3},{6,1},{7,0},{8,15},{9,14},{10,... | collective-permute-start | bytes 221192 | tf_op jit(solution)/shard_map/ppermute | solution.py:31
  8.7 3.4 %collective-permute-start.1 = (f32[48,384]{1,0:T(8,128)S(1)}, f32[48,384]{1,0:T(8,128)S(1)}, u32[]{:S(2)}, u32[]{:S(2)}) collective-permute-start(f32[48,384]{1,0:T(8,128)S(1)} %get-tuple-element.12), channel_id=1, source_target_pairs={{0,1},{1,0},{2,3},{3,2},{4,5},{5,4},{6,7},{7,6},{8,9},{9,8},{10,11... | collective-permute-start | bytes 221192 | tf_op jit(solution)/shard_map/ppermute | solution.py:31
  12.3 5.3 %collective-permute-start.6 = (f32[2,48,128]{2,1,0:T(8,128)S(1)}, f32[2,48,128]{2,1,0:T(8,128)S(1)}, u32[]{:S(2)}, u32[]{:S(2)}) collective-permute-start(f32[2,48,128]{2,1,0:T(8,128)S(1)} %slice.52), channel_id=1, source_target_pairs={{0,17},{1,25},{2,26},{3,18},{4,29},{5,20},{6,31},{7,23},{8,24},{9,... | collective-permute-start | bytes 147464 | tf_op jit(solution)/shard_map/ppermute | solution.py:31
  13.0 5.0 %collective-permute-start.5 = (f32[48,128]{1,0:T(8,128)S(1)}, f32[48,128]{1,0:T(8,128)S(1)}, u32[]{:S(2)}, u32[]{:S(2)}) collective-permute-start(f32[48,128]{1,0:T(8,128)S(1)} %get-tuple-element.14), channel_id=1, source_target_pairs={{0,8},{1,9},{2,10},{3,11},{4,13},{5,12},{6,14},{7,15},{8,0},{9,1},... | collective-permute-start | bytes 73736 | tf_op jit(solution)/shard_map/ppermute | solution.py:31
  17.6 1.2 %collective-permute-start.7 = (f32[48,128]{1,0:T(8,128)S(1)}, f32[48,128]{1,0:T(8,128)S(1)}, u32[]{:S(2)}, u32[]{:S(2)}) collective-permute-start(f32[48,128]{1,0:T(8,128)S(1)} %get-tuple-element.17), channel_id=1, source_target_pairs={{0,1},{1,0},{2,3},{3,2},{4,5},{5,4},{6,7},{7,6},{8,9},{9,8},{10,11... | collective-permute-start | bytes 73736 | tf_op jit(solution)/shard_map/ppermute | solution.py:31

commit v7 on v6

--- a/solution.py
+++ b/solution.py
@@ -6,7 +6,7 @@
 from jax.sharding import PartitionSpec as P
 
 BOTH = ("aux", "occ")
-FLIPS = (((1, 1, 0, 1), (0, 1, 1, 1)), ((0, 0, 1, 0), (0, 0, 0, 1)))
+FLIPS = (((1, 1, 0, 1), (1, 1, 0, 1)), ((0, 0, 1, 0), (0, 0, 0, 0)))
 FLIP_BITS = sum(FLIPS[x][y][z] << (x * 8 + y * 4 + z) for x in range(2) for y in range(2) for z in range(4))
 PLANE = ((1, 0, 0), (1, 1, 0))
 FIRST = (0, 1, 0)
@@ -42,31 +42,26 @@
     blk = nbasis // nblocks
     rows, cols = nbasis // 8, nbasis // 4
 
-    step = ground.shape[0] // 1
-    parts = [pl.ds(k * step, step) for k in range(1)]
-    firsts = [pltpu.make_async_copy(ground_hbm.at[here], ground.at[here], sems.at[3 + k]) for k, here in enumerate(parts)]
-    second = pltpu.make_async_copy(response_hbm, response, sems.at[0])
-    masks = pltpu.make_async_copy(pattern_hbm, pattern, sems.at[1])
-    for first in firsts:
-        first.start()
+    first = pltpu.make_async_copy(ground_hbm, ground, sems.at[0])
+    second = pltpu.make_async_copy(response_hbm, response, sems.at[1])
+    masks = pltpu.make_async_copy(pattern_hbm, pattern, sems.at[2])
+    first.start()
     second.start()
     masks.start()
     x, y, z, core = place()
     kind = core ^ (FLIP_BITS >> (x * 8 + y * 4 + z)) & 1
-    for first, here in zip(firsts, parts):
-        first.wait()
-        turned[:, here] = ground[here, :].T
+    first.wait()
+    turned[...] = ground[...].T
     second.wait()
     masks.wait()
-    block = lax.dot_general(turned[0:128, :], response[...], (((1,), (0,)), ((), ())), preferred_element_type=jnp.float32)
-    for j in range(3):
-        product[0:128, 128 * j : 128 * j + 128] = 0.5 * pattern[0, j].astype(jnp.float32) * block[:, 128 * j : 128 * j + 128]
-    block = lax.dot_general(turned[128:256, :], response[...], (((1,), (0,)), ((), ())), preferred_element_type=jnp.float32)
-    for j in range(3):
-        product[128:256, 128 * j : 128 * j + 128] = 0.5 * pattern[1, j].astype(jnp.float32) * block[:, 128 * j : 128 * j + 128]
-    block = lax.dot_general(turned[256:384, :], response[...], (((1,), (0,)), ((), ())), preferred_element_type=jnp.float32)
-    for j in range(3):
-        product[256:384, 128 * j : 128 * j + 128] = 0.5 * pattern[2, j].astype(jnp.float32) * block[:, 128 * j : 128 * j + 128]
+    for i in range(nblocks):
+        at_i = slice(i * blk, (i + 1) * blk)
+        block = lax.dot_general(
+            turned[at_i, :], response[...], (((1,), (0,)), ((), ())), preferred_element_type=jnp.float32
+        )
+        for j in range(nblocks):
+            at_j = slice(j * blk, (j + 1) * blk)
+            product[at_i, at_j] = 0.5 * pattern[i, j].astype(jnp.float32) * block[:, at_j]
     for i in range(nblocks):
         for j in range(nblocks):
             at_i, at_j = slice(i * blk, (i + 1) * blk), slice(j * blk, (j + 1) * blk)
@@ -142,7 +137,7 @@
             pltpu.VMEM((nbasis, nbasis), jnp.float32),
             pltpu.VMEM((nbasis, nbasis), jnp.float32),
             pltpu.VMEM((nbasis, depth), jnp.bfloat16),
-            pltpu.SemaphoreType.DMA((4,)),
+            pltpu.SemaphoreType.DMA((3,)),
         ],
         compiler_params=params,
     )(*(pltpu.with_memory_space_constraint(a, pltpu.HBM) for a in inputs))

time: 19.8 us -> 19.4 us (0.980)
  the two profiles are of different devices: /device:TPU:7 before, /device:TPU:3 now
where the time goes in v7:
time: 19.4 us; the launch traced here: 19.3 us
  starting transfers between devices  9.51 us (49%)
  waiting for transfers between devices  6.28 us (32%)
  Pallas kernels  3.37 us (17%)
    ppermute x8, starting transfers between devices, swap(): return lax.ppermute(value, BOTH, pairs(moves))  9.51 us
    ppermute x8, waiting for transfers between devices, swap(): return lax.ppermute(value, BOTH, pairs(moves))  6.28 us
    pallas_call x1, Pallas kernels, fast_shards(): pl.pallas_call(product_kernel, out_shape=jax.ShapeDtypeStruct((8, rows, n...  2.48 us
    pallas_call x1, Pallas kernels, fast_shards(): pl.pallas_call(turn_kernel, out_shape=jax.ShapeDtypeStruct((rows, cols),...  0.77 us
  transfers between devices with their start and end apart: 8, of which 4 were waited for; matrix products, arithmetic and copies ran while one was open for 0% of the time, Pallas kernels for 0%

profile of v7, /device:TPU:3, one launch (start us, length us, event | category | flops | bytes accessed | tf_op | source)
XLA Modules:
  0.0 19.3 jit_solution(14780816525354576765)
XLA Ops:
  0.0 2.5 %shard_map.37 = f32[8,48,384]{2,1,0:T(8,128)S(1)} custom-call(s32[3,3]{1,0:T(4,128)} %pattern_hbm.1, bf16[1024,384]{1,0:T(8,128)(2,1)} %bitcast.14, bf16[1024,384]{1,0:T(8,128)(2,1)} %bitcast.15), custom_call_target="tpu_custom_call" | custom-call | tf_op jit(solution)/shard_map/pallas_call | solution.py:128
  2.5 0.7 %collective-permute-start.2 = (f32[2,48,384]{2,1,0:T(8,128)S(1)}, f32[2,48,384]{2,1,0:T(8,128)S(1)}, u32[]{:S(2)}, u32[]{:S(2)}) collective-permute-start(f32[2,48,384]{2,1,0:T(8,128)S(1)} %get-tuple-element.9), channel_id=1, source_target_pairs={{0,1},{1,0},{2,3},{3,2},{4,5},{5,4},{6,7},{7,6},{8,9},{9,8},{10,11... | collective-permute-start | bytes 442376 | tf_op jit(solution)/shard_map/ppermute | solution.py:31
  3.3 1.3 %collective-permute-start = (f32[2,48,384]{2,1,0:T(8,128)S(1)}, f32[2,48,384]{2,1,0:T(8,128)S(1)}, u32[]{:S(2)}, u32[]{:S(2)}) collective-permute-start(f32[2,48,384]{2,1,0:T(8,128)S(1)} %get-tuple-element.11), channel_id=1, source_target_pairs={{0,4},{1,5},{2,6},{3,7},{4,0},{5,1},{6,2},{7,3},{8,12},{9,13},{10,... | collective-permute-start | bytes 442376 | tf_op jit(solution)/shard_map/ppermute | solution.py:31
  4.5 0.0 collective-permute-done.2.came_ref
  4.5 0.6 %collective-permute-start.3 = (f32[48,384]{1,0:T(8,128)S(1)}, f32[48,384]{1,0:T(8,128)S(1)}, u32[]{:S(2)}, u32[]{:S(2)}) collective-permute-start(f32[48,384]{1,0:T(8,128)S(1)} %get-tuple-element.7), channel_id=1, source_target_pairs={{0,3},{1,2},{2,1},{3,0},{4,7},{5,6},{6,5},{7,4},{8,11},{9,10},{10,... | collective-permute-start | bytes 221192 | tf_op jit(solution)/shard_map/ppermute | solution.py:31
  5.1 2.0 %collective-permute-start.4 = (f32[48,384]{1,0:T(8,128)S(1)}, f32[48,384]{1,0:T(8,128)S(1)}, u32[]{:S(2)}, u32[]{:S(2)}) collective-permute-start(f32[48,384]{1,0:T(8,128)S(1)} %get-tuple-element.8), channel_id=1, source_target_pairs={{0,7},{1,6},{2,5},{3,4},{4,3},{5,2},{6,1},{7,0},{8,15},{9,14},{10,... | collective-permute-start | bytes 221192 | tf_op jit(solution)/shard_map/ppermute | solution.py:31
  7.1 1.6 %collective-permute-done = f32[2,48,384]{2,1,0:T(8,128)S(1)} collective-permute-done((f32[2,48,384]{2,1,0:T(8,128)S(1)}, f32[2,48,384]{2,1,0:T(8,128)S(1)}, u32[]{:S(2)}, u32[]{:S(2)}) %collective-permute-start) | collective-permute-done | bytes 147488 | tf_op jit(solution)/shard_map/ppermute | solution.py:31
  8.7 0.9 %collective-permute-start.1 = (f32[48,384]{1,0:T(8,128)S(1)}, f32[48,384]{1,0:T(8,128)S(1)}, u32[]{:S(2)}, u32[]{:S(2)}) collective-permute-start(f32[48,384]{1,0:T(8,128)S(1)} %get-tuple-element.12), channel_id=1, source_target_pairs={{0,1},{1,0},{2,3},{3,2},{4,5},{5,4},{6,7},{7,6},{8,9},{9,8},{10,11... | collective-permute-start | bytes 221192 | tf_op jit(solution)/shard_map/ppermute | solution.py:31
  9.7 0.0 collective-permute-done.3.b_ref
  9.7 1.5 %collective-permute-done.4.c_ref = f32[48,384]{1,0:T(8,128)S(1)} collective-permute-done((f32[48,384]{1,0:T(8,128)S(1)}, f32[48,384]{1,0:T(8,128)S(1)}, u32[]{:S(2)}, u32[]{:S(2)}) %collective-permute-start.4) | collective-permute-done | bytes 73760 | tf_op jit(solution)/shard_map/ppermute | solution.py:31
  11.1 0.0 collective-permute-done.1.a_ref
  11.1 0.1 shard_map.39
  11.3 2.0 %collective-permute-start.6 = (f32[2,48,128]{2,1,0:T(8,128)S(1)}, f32[2,48,128]{2,1,0:T(8,128)S(1)}, u32[]{:S(2)}, u32[]{:S(2)}) collective-permute-start(f32[2,48,128]{2,1,0:T(8,128)S(1)} %slice.52), channel_id=1, source_target_pairs={{0,17},{1,25},{2,26},{3,18},{4,21},{5,29},{6,30},{7,23},{8,24},{9,... | collective-permute-start | bytes 147464 | tf_op jit(solution)/shard_map/ppermute | solution.py:31
  13.3 1.6 %collective-permute-start.5 = (f32[48,128]{1,0:T(8,128)S(1)}, f32[48,128]{1,0:T(8,128)S(1)}, u32[]{:S(2)}, u32[]{:S(2)}) collective-permute-start(f32[48,128]{1,0:T(8,128)S(1)} %get-tuple-element.14), channel_id=1, source_target_pairs={{0,8},{1,9},{2,10},{3,11},{4,12},{5,13},{6,14},{7,15},{8,0},{9,1},... | collective-permute-start | bytes 73736 | tf_op jit(solution)/shard_map/ppermute | solution.py:31
  14.9 2.3 %collective-permute-done.6 = f32[2,48,128]{2,1,0:T(8,128)S(1)} collective-permute-done((f32[2,48,128]{2,1,0:T(8,128)S(1)}, f32[2,48,128]{2,1,0:T(8,128)S(1)}, u32[]{:S(2)}, u32[]{:S(2)}) %collective-permute-start.6) | collective-permute-done | bytes 49184 | tf_op jit(solution)/shard_map/ppermute | solution.py:31
  17.3 0.4 %collective-permute-start.7 = (f32[48,128]{1,0:T(8,128)S(1)}, f32[48,128]{1,0:T(8,128)S(1)}, u32[]{:S(2)}, u32[]{:S(2)}) collective-permute-start(f32[48,128]{1,0:T(8,128)S(1)} %get-tuple-element.17), channel_id=1, source_target_pairs={{0,1},{1,0},{2,3},{3,2},{4,5},{5,4},{6,7},{7,6},{8,9},{9,8},{10,11... | collective-permute-start | bytes 73736 | tf_op jit(solution)/shard_map/ppermute | solution.py:31
  17.7 0.0 collective-permute-done.5.a_ref
  17.7 0.8 %collective-permute-done.7.b_ref = f32[48,128]{1,0:T(8,128)S(1)} collective-permute-done((f32[48,128]{1,0:T(8,128)S(1)}, f32[48,128]{1,0:T(8,128)S(1)}, u32[]{:S(2)}, u32[]{:S(2)}) %collective-permute-start.7) | collective-permute-done | bytes 24608 | tf_op jit(solution)/shard_map/ppermute | solution.py:31
  18.5 0.8 %shard_map.40 = f32[48,96]{1,0:T(8,128)} custom-call(f32[48,128]{1,0:T(8,128)S(1)} %get-tuple-element.15.own_ref, f32[48,128]{1,0:T(8,128)S(1)} %collective-permute-done.5.a_ref, f32[48,128]{1,0:T(8,128)S(1)} %collective-permute-done.7.b_ref, f32[48,128]{1,0:T(8,128)S(1)} %get-tuple-element.16.c_ref), custom_call_target="tpu_custom_call" | custom-call | tf_op jit(solution)/shard_map/pallas_call | solution.py:166
  (7 shorter events, 0.1 us)
Async XLA Ops:
  2.5 2.0 %collective-permute-start.2 = (f32[2,48,384]{2,1,0:T(8,128)S(1)}, f32[2,48,384]{2,1,0:T(8,128)S(1)}, u32[]{:S(2)}, u32[]{:S(2)}) collective-permute-start(f32[2,48,384]{2,1,0:T(8,128)S(1)} %get-tuple-element.9), channel_id=1, source_target_pairs={{0,1},{1,0},{2,3},{3,2},{4,5},{5,4},{6,7},{7,6},{8,9},{9,8},{10,11... | collective-permute-start | bytes 442376 | tf_op jit(solution)/shard_map/ppermute | solution.py:31
  3.3 5.4 %collective-permute-start = (f32[2,48,384]{2,1,0:T(8,128)S(1)}, f32[2,48,384]{2,1,0:T(8,128)S(1)}, u32[]{:S(2)}, u32[]{:S(2)}) collective-permute-start(f32[2,48,384]{2,1,0:T(8,128)S(1)} %get-tuple-element.11), channel_id=1, source_target_pairs={{0,4},{1,5},{2,6},{3,7},{4,0},{5,1},{6,2},{7,3},{8,12},{9,13},{10,... | collective-permute-start | bytes 442376 | tf_op jit(solution)/shard_map/ppermute | solution.py:31
  4.5 5.1 %collective-permute-start.3 = (f32[48,384]{1,0:T(8,128)S(1)}, f32[48,384]{1,0:T(8,128)S(1)}, u32[]{:S(2)}, u32[]{:S(2)}) collective-permute-start(f32[48,384]{1,0:T(8,128)S(1)} %get-tuple-element.7), channel_id=1, source_target_pairs={{0,3},{1,2},{2,1},{3,0},{4,7},{5,6},{6,5},{7,4},{8,11},{9,10},{10,... | collective-permute-start | bytes 221192 | tf_op jit(solution)/shard_map/ppermute | solution.py:31
  5.1 6.0 %collective-permute-start.4 = (f32[48,384]{1,0:T(8,128)S(1)}, f32[48,384]{1,0:T(8,128)S(1)}, u32[]{:S(2)}, u32[]{:S(2)}) collective-permute-start(f32[48,384]{1,0:T(8,128)S(1)} %get-tuple-element.8), channel_id=1, source_target_pairs={{0,7},{1,6},{2,5},{3,4},{4,3},{5,2},{6,1},{7,0},{8,15},{9,14},{10,... | collective-permute-start | bytes 221192 | tf_op jit(solution)/shard_map/ppermute | solution.py:31
  8.7 2.4 %collective-permute-start.1 = (f32[48,384]{1,0:T(8,128)S(1)}, f32[48,384]{1,0:T(8,128)S(1)}, u32[]{:S(2)}, u32[]{:S(2)}) collective-permute-start(f32[48,384]{1,0:T(8,128)S(1)} %get-tuple-element.12), channel_id=1, source_target_pairs={{0,1},{1,0},{2,3},{3,2},{4,5},{5,4},{6,7},{7,6},{8,9},{9,8},{10,11... | collective-permute-start | bytes 221192 | tf_op jit(solution)/shard_map/ppermute | solution.py:31
  11.3 6.0 %collective-permute-start.6 = (f32[2,48,128]{2,1,0:T(8,128)S(1)}, f32[2,48,128]{2,1,0:T(8,128)S(1)}, u32[]{:S(2)}, u32[]{:S(2)}) collective-permute-start(f32[2,48,128]{2,1,0:T(8,128)S(1)} %slice.52), channel_id=1, source_target_pairs={{0,17},{1,25},{2,26},{3,18},{4,21},{5,29},{6,30},{7,23},{8,24},{9,... | collective-permute-start | bytes 147464 | tf_op jit(solution)/shard_map/ppermute | solution.py:31
  13.3 4.4 %collective-permute-start.5 = (f32[48,128]{1,0:T(8,128)S(1)}, f32[48,128]{1,0:T(8,128)S(1)}, u32[]{:S(2)}, u32[]{:S(2)}) collective-permute-start(f32[48,128]{1,0:T(8,128)S(1)} %get-tuple-element.14), channel_id=1, source_target_pairs={{0,8},{1,9},{2,10},{3,11},{4,12},{5,13},{6,14},{7,15},{8,0},{9,1},... | collective-permute-start | bytes 73736 | tf_op jit(solution)/shard_map/ppermute | solution.py:31
  17.3 1.2 %collective-permute-start.7 = (f32[48,128]{1,0:T(8,128)S(1)}, f32[48,128]{1,0:T(8,128)S(1)}, u32[]{:S(2)}, u32[]{:S(2)}) collective-permute-start(f32[48,128]{1,0:T(8,128)S(1)} %get-tuple-element.17), channel_id=1, source_target_pairs={{0,1},{1,0},{2,3},{3,2},{4,5},{5,4},{6,7},{7,6},{8,9},{9,8},{10,11... | collective-permute-start | bytes 73736 | tf_op jit(solution)/shard_map/ppermute | solution.py:31

commit v8 on v7

--- a/solution.py
+++ b/solution.py
@@ -6,7 +6,7 @@
 from jax.sharding import PartitionSpec as P
 
 BOTH = ("aux", "occ")
-FLIPS = (((1, 1, 0, 1), (1, 1, 0, 1)), ((0, 0, 1, 0), (0, 0, 0, 0)))
+FLIPS = (((1, 0, 0, 1), (1, 1, 0, 1)), ((0, 0, 1, 0), (0, 0, 0, 1)))
 FLIP_BITS = sum(FLIPS[x][y][z] << (x * 8 + y * 4 + z) for x in range(2) for y in range(2) for z in range(4))
 PLANE = ((1, 0, 0), (1, 1, 0))
 FIRST = (0, 1, 0)
@@ -54,14 +54,15 @@
     turned[...] = ground[...].T
     second.wait()
     masks.wait()
-    for i in range(nblocks):
-        at_i = slice(i * blk, (i + 1) * blk)
-        block = lax.dot_general(
-            turned[at_i, :], response[...], (((1,), (0,)), ((), ())), preferred_element_type=jnp.float32
-        )
-        for j in range(nblocks):
-            at_j = slice(j * blk, (j + 1) * blk)
-            product[at_i, at_j] = 0.5 * pattern[i, j].astype(jnp.float32) * block[:, at_j]
+    block = lax.dot_general(turned[0:128, :], response[...], (((1,), (0,)), ((), ())), preferred_element_type=jnp.float32)
+    for j in range(3):
+        product[0:128, 128 * j : 128 * j + 128] = 0.5 * pattern[0, j].astype(jnp.float32) * block[:, 128 * j : 128 * j + 128]
+    block = lax.dot_general(turned[128:256, :], response[...], (((1,), (0,)), ((), ())), preferred_element_type=jnp.float32)
+    for j in range(3):
+        product[128:256, 128 * j : 128 * j + 128] = 0.5 * pattern[1, j].astype(jnp.float32) * block[:, 128 * j : 128 * j + 128]
+    block = lax.dot_general(turned[256:384, :], response[...], (((1,), (0,)), ((), ())), preferred_element_type=jnp.float32)
+    for j in range(3):
+        product[256:384, 128 * j : 128 * j + 128] = 0.5 * pattern[2, j].astype(jnp.float32) * block[:, 128 * j : 128 * j + 128]
     for i in range(nblocks):
         for j in range(nblocks):
             at_i, at_j = slice(i * blk, (i + 1) * blk), slice(j * blk, (j + 1) * blk)
@@ -100,20 +101,46 @@
     y_ref[...] = own_ref[1] + came_ref[1]
 
 
-def split_kernel(own_ref, a_ref, b_ref, c_ref, out_ref):
-    cols = own_ref.shape[1] // 4
+def split_kernel(own_ref, a_ref, b_ref, c_ref, tile_ref, far_ref):
+    rows, nbasis = own_ref.shape
+    cols, half = nbasis // 4, rows // 2
     total = own_ref[...] + a_ref[...] + b_ref[...] + c_ref[...]
     x, y, z, core = place()
-    kind = core ^ (FLIP_BITS >> (x * 8 + y * 4 + z)) & 1
     for z_to in range(4):
-        turn = z ^ z_to
-        slot = jnp.where((turn >= 2) & (kind == 0), 5 - turn, turn)
-        out_ref[slot, :, :cols] = total[:, cols * z_to : cols * (z_to + 1)]
-
-
-def turn_kernel(own_ref, a_ref, b_ref, c_ref, out_ref):
+        tile_ref[jnp.minimum(z ^ z_to, 2), :, :cols] = total[:, cols * z_to : cols * (z_to + 1)]
+    turned = pltpu.roll(total, nbasis // 2, 1)
+    lane = lax.broadcasted_iota(jnp.int32, (half, nbasis), 1)
+    low = lane < nbasis // 2
+    high_far = jnp.full_like(lane, z // 2) == 0
+    far_ref[...] = jnp.where(
+        high_far, jnp.where(low, turned[:half], total[half:]), jnp.where(low, total[:half], turned[half:])
+    )
+
+
+def part_of(far_ref, parity):
+    half, nbasis = far_ref.shape
+    cols = nbasis // 4
+    x, y, z, core = place()
+    odd = jnp.full(far_ref.shape, (z ^ parity) & 1) == 1
+    far = jnp.where(odd, pltpu.roll(far_ref[...], 3 * cols, 1), far_ref[...])
+    return far[:, :cols], far[:, 2 * cols : 3 * cols]
+
+
+def pick_kernel(far_ref, out_ref):
+    half, cols = far_ref.shape[0], far_ref.shape[1] // 4
+    out_ref[:half, :cols], out_ref[half:, :cols] = part_of(far_ref, 1)
+
+
+def home_kernel(home_ref, far_ref, out_ref):
+    half, cols = far_ref.shape[0], far_ref.shape[1] // 4
+    top, bottom = part_of(far_ref, 0)
+    out_ref[:half, :cols] = home_ref[:half, :cols] + top
+    out_ref[half:, :cols] = home_ref[half:, :cols] + bottom
+
+
+def turn_kernel(home_ref, near_ref, other_ref, out_ref):
     rows, cols = out_ref.shape
-    total = own_ref[...] + a_ref[...] + b_ref[...] + c_ref[...]
+    total = home_ref[...] + near_ref[...] + other_ref[...]
     turned = total[:, :cols].T
     out_ref[...] = jnp.concatenate([turned[:rows], turned[rows:]], axis=1)
 
@@ -154,22 +181,41 @@
     near = [swap(sides[move[1]], move, move) for move in PLANE]
     own = parts[0:2] + first
     plane = [swap(own[1]), *near]
-    line = pl.pallas_call(
+    line, far = pl.pallas_call(
         split_kernel,
-        out_shape=jax.ShapeDtypeStruct((4, rows, 128), jnp.float32),
+        out_shape=(
+            jax.ShapeDtypeStruct((3, rows, 128), jnp.float32),
+            jax.ShapeDtypeStruct((rows // 2, nbasis), jnp.float32),
+        ),
         in_specs=[vmem] * 4,
-        out_specs=vmem,
+        out_specs=(vmem, vmem),
         compiler_params=params,
     )(own[0], *plane)
-    far = swap(line[2:], *FAR)
-    last = [swap(line[1], NEAR, NEAR), swap(far[1]), far[0]]
+    far = swap(far, *FAR)
+    near = swap(line[1], NEAR, NEAR)
+    other = pl.pallas_call(
+        pick_kernel,
+        out_shape=jax.ShapeDtypeStruct((rows, 128), jnp.float32),
+        in_specs=[vmem],
+        out_specs=vmem,
+        cost_estimate=pl.CostEstimate(flops=100_000, bytes_accessed=600_000, transcendentals=0),
+        compiler_params=params,
+    )(far)
+    home = pl.pallas_call(
+        home_kernel,
+        out_shape=jax.ShapeDtypeStruct((rows, 128), jnp.float32),
+        in_specs=[vmem] * 2,
+        out_specs=vmem,
+        cost_estimate=pl.CostEstimate(flops=100_000, bytes_accessed=600_000, transcendentals=0),
+        compiler_params=params,
+    )(line[0], far)
     return pl.pallas_call(
         turn_kernel,
         out_shape=jax.ShapeDtypeStruct((rows, cols), jnp.float32),
-        in_specs=[vmem] * 4,
-        out_specs=vmem,
-        compiler_params=params,
-    )(line[0], *last)
+        in_specs=[vmem] * 3,
+        out_specs=vmem,
+        compiler_params=params,
+    )(home, near, swap(other))
 
 
 def any_shards(factors, response, pattern):

time: 19.4 us -> 19.4 us (level)
  the two profiles are of different devices: /device:TPU:3 before, /device:TPU:1 now
where the time goes in v8:
time: 19.4 us; the launch traced here: 19.2 us
  starting transfers between devices  9.51 us (49%)
  waiting for transfers between devices  5.92 us (31%)
  Pallas kernels  3.66 us (19%)
    ppermute x8, starting transfers between devices, swap(): return lax.ppermute(value, BOTH, pairs(moves))  9.51 us
    ppermute x8, waiting for transfers between devices, swap(): return lax.ppermute(value, BOTH, pairs(moves))  5.92 us
    pallas_call x1, Pallas kernels, fast_shards(): pl.pallas_call(product_kernel, out_shape=jax.ShapeDtypeStruct((8, rows, n...  2.48 us
    pallas_call x1, Pallas kernels, fast_shards(): pl.pallas_call(turn_kernel, out_shape=jax.ShapeDtypeStruct((rows, cols),...  0.77 us
  transfers between devices with their start and end apart: 8, of which 4 were waited for; matrix products, arithmetic and copies ran while one was open for 0% of the time, Pallas kernels for 2%

profile of v8, /device:TPU:1, one launch (start us, length us, event | category | flops | bytes accessed | tf_op | source)
XLA Modules:
  0.0 19.2 jit_solution(11507439623487846079)
XLA Ops:
  0.0 2.5 %shard_map.37 = f32[8,48,384]{2,1,0:T(8,128)S(1)} custom-call(s32[3,3]{1,0:T(4,128)} %pattern_hbm.1, bf16[1024,384]{1,0:T(8,128)(2,1)} %bitcast.10, bf16[1024,384]{1,0:T(8,128)(2,1)} %bitcast.11), custom_call_target="tpu_custom_call" | custom-call | tf_op jit(solution)/shard_map/pallas_call | solution.py:155
  2.5 0.1 collective-permute-start.2
  2.7 2.7 %collective-permute-start = (f32[2,48,384]{2,1,0:T(8,128)S(1)}, f32[2,48,384]{2,1,0:T(8,128)S(1)}, u32[]{:S(2)}, u32[]{:S(2)}) collective-permute-start(f32[2,48,384]{2,1,0:T(8,128)S(1)} %get-tuple-element.15), channel_id=1, source_target_pairs={{0,4},{1,5},{2,6},{3,7},{4,0},{5,1},{6,2},{7,3},{8,13},{9,12},{10,... | collective-permute-start | bytes 442376 | tf_op jit(solution)/shard_map/ppermute | solution.py:31
  5.4 0.0 collective-permute-done.2.came_ref
  5.4 1.5 %collective-permute-start.3 = (f32[48,384]{1,0:T(8,128)S(1)}, f32[48,384]{1,0:T(8,128)S(1)}, u32[]{:S(2)}, u32[]{:S(2)}) collective-permute-start(f32[48,384]{1,0:T(8,128)S(1)} %get-tuple-element.9), channel_id=1, source_target_pairs={{0,3},{1,2},{2,1},{3,0},{4,7},{5,6},{6,5},{7,4},{8,10},{9,11},{10,... | collective-permute-start | bytes 221192 | tf_op jit(solution)/shard_map/ppermute | solution.py:31
  6.9 1.0 %collective-permute-start.4 = (f32[48,384]{1,0:T(8,128)S(1)}, f32[48,384]{1,0:T(8,128)S(1)}, u32[]{:S(2)}, u32[]{:S(2)}) collective-permute-start(f32[48,384]{1,0:T(8,128)S(1)} %get-tuple-element.10), channel_id=1, source_target_pairs={{0,7},{1,6},{2,5},{3,4},{4,3},{5,2},{6,1},{7,0},{8,14},{9,15},{10,... | collective-permute-start | bytes 221192 | tf_op jit(solution)/shard_map/ppermute | solution.py:31
  7.9 1.6 %collective-permute-done = f32[2,48,384]{2,1,0:T(8,128)S(1)} collective-permute-done((f32[2,48,384]{2,1,0:T(8,128)S(1)}, f32[2,48,384]{2,1,0:T(8,128)S(1)}, u32[]{:S(2)}, u32[]{:S(2)}) %collective-permute-start) | collective-permute-done | bytes 147488 | tf_op jit(solution)/shard_map/ppermute | solution.py:31
  9.5 0.7 %collective-permute-start.1 = (f32[48,384]{1,0:T(8,128)S(1)}, f32[48,384]{1,0:T(8,128)S(1)}, u32[]{:S(2)}, u32[]{:S(2)}) collective-permute-start(f32[48,384]{1,0:T(8,128)S(1)} %get-tuple-element.16), channel_id=1, source_target_pairs={{0,1},{1,0},{2,3},{3,2},{4,5},{5,4},{6,7},{7,6},{8,9},{9,8},{10,11... | collective-permute-start | bytes 221192 | tf_op jit(solution)/shard_map/ppermute | solution.py:31
  10.2 0.0 collective-permute-done.3.b_ref
  10.2 1.7 %collective-permute-done.4.c_ref = f32[48,384]{1,0:T(8,128)S(1)} collective-permute-done((f32[48,384]{1,0:T(8,128)S(1)}, f32[48,384]{1,0:T(8,128)S(1)}, u32[]{:S(2)}, u32[]{:S(2)}) %collective-permute-start.4) | collective-permute-done | bytes 73760 | tf_op jit(solution)/shard_map/ppermute | solution.py:31
  12.0 0.0 collective-permute-done.1.a_ref
  12.0 0.1 shard_map.39
  12.1 3.1 %collective-permute-start.5 = (f32[24,384]{1,0:T(8,128)S(1)}, f32[24,384]{1,0:T(8,128)S(1)}, u32[]{:S(2)}, u32[]{:S(2)}) collective-permute-start(f32[24,384]{1,0:T(8,128)S(1)} %get-tuple-element.12), channel_id=1, source_target_pairs={{0,17},{1,25},{2,26},{3,18},{4,21},{5,29},{6,31},{7,23},{8,16},{9,... | collective-permute-start | bytes 110600 | tf_op jit(solution)/shard_map/ppermute | solution.py:31
  15.2 0.3 %collective-permute-start.6 = (f32[48,128]{1,0:T(8,128)S(1)}, f32[48,128]{1,0:T(8,128)S(1)}, u32[]{:S(2)}, u32[]{:S(2)}) collective-permute-start(f32[48,128]{1,0:T(8,128)S(1)} %get-tuple-element.18), channel_id=1, source_target_pairs={{0,9},{1,8},{2,10},{3,11},{4,12},{5,13},{6,14},{7,15},{8,1},{9,0},... | collective-permute-start | bytes 73736 | tf_op jit(solution)/shard_map/ppermute | solution.py:31
  15.5 1.3 %collective-permute-done.5.far_ref = f32[24,384]{1,0:T(8,128)S(1)} collective-permute-done((f32[24,384]{1,0:T(8,128)S(1)}, f32[24,384]{1,0:T(8,128)S(1)}, u32[]{:S(2)}, u32[]{:S(2)}) %collective-permute-start.5) | collective-permute-done | bytes 36896 | tf_op jit(solution)/shard_map/ppermute | solution.py:31
  16.8 0.1 shard_map.41
  16.9 0.1 collective-permute-start.7
  17.0 0.1 shard_map.40.home_ref
  17.1 1.3 %collective-permute-done.6.near_ref = f32[48,128]{1,0:T(8,128)S(1)} collective-permute-done((f32[48,128]{1,0:T(8,128)S(1)}, f32[48,128]{1,0:T(8,128)S(1)}, u32[]{:S(2)}, u32[]{:S(2)}) %collective-permute-start.6) | collective-permute-done | bytes 24608 | tf_op jit(solution)/shard_map/ppermute | solution.py:31
  18.4 0.0 collective-permute-done.7.other_ref
  18.4 0.8 %shard_map.42 = f32[48,96]{1,0:T(8,128)} custom-call(f32[48,128]{1,0:T(8,128)S(1)} %shard_map.40.home_ref, f32[48,128]{1,0:T(8,128)S(1)} %collective-permute-done.6.near_ref, f32[48,128]{1,0:T(8,128)S(1)} %collective-permute-done.7.other_ref), custom_call_target="tpu_custom_call" | custom-call | tf_op jit(solution)/shard_map/pallas_call | solution.py:212
  (5 shorter events, 0.1 us)
Async XLA Ops:
  2.5 2.8 %collective-permute-start.2 = (f32[2,48,384]{2,1,0:T(8,128)S(1)}, f32[2,48,384]{2,1,0:T(8,128)S(1)}, u32[]{:S(2)}, u32[]{:S(2)}) collective-permute-start(f32[2,48,384]{2,1,0:T(8,128)S(1)} %get-tuple-element.13), channel_id=1, source_target_pairs={{0,1},{1,0},{2,3},{3,2},{4,5},{5,4},{6,7},{7,6},{8,9},{9,8},{10,11... | collective-permute-start | bytes 442376 | tf_op jit(solution)/shard_map/ppermute | solution.py:31
  2.7 6.8 %collective-permute-start = (f32[2,48,384]{2,1,0:T(8,128)S(1)}, f32[2,48,384]{2,1,0:T(8,128)S(1)}, u32[]{:S(2)}, u32[]{:S(2)}) collective-permute-start(f32[2,48,384]{2,1,0:T(8,128)S(1)} %get-tuple-element.15), channel_id=1, source_target_pairs={{0,4},{1,5},{2,6},{3,7},{4,0},{5,1},{6,2},{7,3},{8,13},{9,12},{10,... | collective-permute-start | bytes 442376 | tf_op jit(solution)/shard_map/ppermute | solution.py:31
  5.4 4.9 %collective-permute-start.3 = (f32[48,384]{1,0:T(8,128)S(1)}, f32[48,384]{1,0:T(8,128)S(1)}, u32[]{:S(2)}, u32[]{:S(2)}) collective-permute-start(f32[48,384]{1,0:T(8,128)S(1)} %get-tuple-element.9), channel_id=1, source_target_pairs={{0,3},{1,2},{2,1},{3,0},{4,7},{5,6},{6,5},{7,4},{8,10},{9,11},{10,... | collective-permute-start | bytes 221192 | tf_op jit(solution)/shard_map/ppermute | solution.py:31
  6.9 5.1 %collective-permute-start.4 = (f32[48,384]{1,0:T(8,128)S(1)}, f32[48,384]{1,0:T(8,128)S(1)}, u32[]{:S(2)}, u32[]{:S(2)}) collective-permute-start(f32[48,384]{1,0:T(8,128)S(1)} %get-tuple-element.10), channel_id=1, source_target_pairs={{0,7},{1,6},{2,5},{3,4},{4,3},{5,2},{6,1},{7,0},{8,14},{9,15},{10,... | collective-permute-start | bytes 221192 | tf_op jit(solution)/shard_map/ppermute | solution.py:31
  9.5 2.5 %collective-permute-start.1 = (f32[48,384]{1,0:T(8,128)S(1)}, f32[48,384]{1,0:T(8,128)S(1)}, u32[]{:S(2)}, u32[]{:S(2)}) collective-permute-start(f32[48,384]{1,0:T(8,128)S(1)} %get-tuple-element.16), channel_id=1, source_target_pairs={{0,1},{1,0},{2,3},{3,2},{4,5},{5,4},{6,7},{7,6},{8,9},{9,8},{10,11... | collective-permute-start | bytes 221192 | tf_op jit(solution)/shard_map/ppermute | solution.py:31
  12.1 4.7 %collective-permute-start.5 = (f32[24,384]{1,0:T(8,128)S(1)}, f32[24,384]{1,0:T(8,128)S(1)}, u32[]{:S(2)}, u32[]{:S(2)}) collective-permute-start(f32[24,384]{1,0:T(8,128)S(1)} %get-tuple-element.12), channel_id=1, source_target_pairs={{0,17},{1,25},{2,26},{3,18},{4,21},{5,29},{6,31},{7,23},{8,16},{9,... | collective-permute-start | bytes 110600 | tf_op jit(solution)/shard_map/ppermute | solution.py:31
  15.2 3.3 %collective-permute-start.6 = (f32[48,128]{1,0:T(8,128)S(1)}, f32[48,128]{1,0:T(8,128)S(1)}, u32[]{:S(2)}, u32[]{:S(2)}) collective-permute-start(f32[48,128]{1,0:T(8,128)S(1)} %get-tuple-element.18), channel_id=1, source_target_pairs={{0,9},{1,8},{2,10},{3,11},{4,12},{5,13},{6,14},{7,15},{8,1},{9,0},... | collective-permute-start | bytes 73736 | tf_op jit(solution)/shard_map/ppermute | solution.py:31
  16.9 1.5 %collective-permute-start.7 = (f32[48,128]{1,0:T(8,128)S(1)}, f32[48,128]{1,0:T(8,128)S(1)}, u32[]{:S(2)}, u32[]{:S(2)}) collective-permute-start(f32[48,128]{1,0:T(8,128)S(1)} %shard_map.41), channel_id=1, source_target_pairs={{0,1},{1,0},{2,3},{3,2},{4,5},{5,4},{6,7},{7,6},{8,9},{9,8},{10,11... | collective-permute-start | bytes 73736 | tf_op jit(solution)/shard_map/ppermute | solution.py:31

commit v9 on v8

--- a/solution.py
+++ b/solution.py
@@ -121,9 +121,9 @@
     half, nbasis = far_ref.shape
     cols = nbasis // 4
     x, y, z, core = place()
-    odd = jnp.full(far_ref.shape, (z ^ parity) & 1) == 1
-    far = jnp.where(odd, pltpu.roll(far_ref[...], 3 * cols, 1), far_ref[...])
-    return far[:, :cols], far[:, 2 * cols : 3 * cols]
+    odd = jnp.full((half, cols), (z ^ parity) & 1) == 1
+    first, second, third, fourth = (far_ref[:, cols * k : cols * (k + 1)] for k in range(4))
+    return jnp.where(odd, second, first), jnp.where(odd, fourth, third)
 
 
 def pick_kernel(far_ref, out_ref):

time: 19.4 us -> 19.4 us (level)
  no operation moved by 1% of the time
where the time goes in v9:
time: 19.4 us; the launch traced here: 19.2 us
  starting transfers between devices  9.51 us (49%)
  waiting for transfers between devices  5.92 us (31%)
  Pallas kernels  3.66 us (19%)
    ppermute x8, starting transfers between devices, swap(): return lax.ppermute(value, BOTH, pairs(moves))  9.51 us
    ppermute x8, waiting for transfers between devices, swap(): return lax.ppermute(value, BOTH, pairs(moves))  5.92 us
    pallas_call x1, Pallas kernels, fast_shards(): pl.pallas_call(product_kernel, out_shape=jax.ShapeDtypeStruct((8, rows, n...  2.48 us
    pallas_call x1, Pallas kernels, fast_shards(): pl.pallas_call(turn_kernel, out_shape=jax.ShapeDtypeStruct((rows, cols),...  0.77 us
  transfers between devices with their start and end apart: 8, of which 4 were waited for; matrix products, arithmetic and copies ran while one was open for 0% of the time, Pallas kernels for 2%

profile of v9, /device:TPU:1, one launch (start us, length us, event | category | flops | bytes accessed | tf_op | source)
XLA Modules:
  0.0 19.2 jit_solution(4469681044430362900)
XLA Ops:
  0.0 2.5 %shard_map.37 = f32[8,48,384]{2,1,0:T(8,128)S(1)} custom-call(s32[3,3]{1,0:T(4,128)} %pattern_hbm.1, bf16[1024,384]{1,0:T(8,128)(2,1)} %bitcast.10, bf16[1024,384]{1,0:T(8,128)(2,1)} %bitcast.11), custom_call_target="tpu_custom_call" | custom-call | tf_op jit(solution)/shard_map/pallas_call | solution.py:155
  2.5 0.1 collective-permute-start.2
  2.7 2.7 %collective-permute-start = (f32[2,48,384]{2,1,0:T(8,128)S(1)}, f32[2,48,384]{2,1,0:T(8,128)S(1)}, u32[]{:S(2)}, u32[]{:S(2)}) collective-permute-start(f32[2,48,384]{2,1,0:T(8,128)S(1)} %get-tuple-element.15), channel_id=1, source_target_pairs={{0,4},{1,5},{2,6},{3,7},{4,0},{5,1},{6,2},{7,3},{8,13},{9,12},{10,... | collective-permute-start | bytes 442376 | tf_op jit(solution)/shard_map/ppermute | solution.py:31
  5.4 0.0 collective-permute-done.2.came_ref
  5.4 1.5 %collective-permute-start.3 = (f32[48,384]{1,0:T(8,128)S(1)}, f32[48,384]{1,0:T(8,128)S(1)}, u32[]{:S(2)}, u32[]{:S(2)}) collective-permute-start(f32[48,384]{1,0:T(8,128)S(1)} %get-tuple-element.9), channel_id=1, source_target_pairs={{0,3},{1,2},{2,1},{3,0},{4,7},{5,6},{6,5},{7,4},{8,10},{9,11},{10,... | collective-permute-start | bytes 221192 | tf_op jit(solution)/shard_map/ppermute | solution.py:31
  6.9 1.0 %collective-permute-start.4 = (f32[48,384]{1,0:T(8,128)S(1)}, f32[48,384]{1,0:T(8,128)S(1)}, u32[]{:S(2)}, u32[]{:S(2)}) collective-permute-start(f32[48,384]{1,0:T(8,128)S(1)} %get-tuple-element.10), channel_id=1, source_target_pairs={{0,7},{1,6},{2,5},{3,4},{4,3},{5,2},{6,1},{7,0},{8,14},{9,15},{10,... | collective-permute-start | bytes 221192 | tf_op jit(solution)/shard_map/ppermute | solution.py:31
  7.9 1.6 %collective-permute-done = f32[2,48,384]{2,1,0:T(8,128)S(1)} collective-permute-done((f32[2,48,384]{2,1,0:T(8,128)S(1)}, f32[2,48,384]{2,1,0:T(8,128)S(1)}, u32[]{:S(2)}, u32[]{:S(2)}) %collective-permute-start) | collective-permute-done | bytes 147488 | tf_op jit(solution)/shard_map/ppermute | solution.py:31
  9.5 0.7 %collective-permute-start.1 = (f32[48,384]{1,0:T(8,128)S(1)}, f32[48,384]{1,0:T(8,128)S(1)}, u32[]{:S(2)}, u32[]{:S(2)}) collective-permute-start(f32[48,384]{1,0:T(8,128)S(1)} %get-tuple-element.16), channel_id=1, source_target_pairs={{0,1},{1,0},{2,3},{3,2},{4,5},{5,4},{6,7},{7,6},{8,9},{9,8},{10,11... | collective-permute-start | bytes 221192 | tf_op jit(solution)/shard_map/ppermute | solution.py:31
  10.2 0.0 collective-permute-done.3.b_ref
  10.2 1.7 %collective-permute-done.4.c_ref = f32[48,384]{1,0:T(8,128)S(1)} collective-permute-done((f32[48,384]{1,0:T(8,128)S(1)}, f32[48,384]{1,0:T(8,128)S(1)}, u32[]{:S(2)}, u32[]{:S(2)}) %collective-permute-start.4) | collective-permute-done | bytes 73760 | tf_op jit(solution)/shard_map/ppermute | solution.py:31
  12.0 0.0 collective-permute-done.1.a_ref
  12.0 0.1 shard_map.39
  12.1 3.1 %collective-permute-start.5 = (f32[24,384]{1,0:T(8,128)S(1)}, f32[24,384]{1,0:T(8,128)S(1)}, u32[]{:S(2)}, u32[]{:S(2)}) collective-permute-start(f32[24,384]{1,0:T(8,128)S(1)} %get-tuple-element.12), channel_id=1, source_target_pairs={{0,17},{1,25},{2,26},{3,18},{4,21},{5,29},{6,31},{7,23},{8,16},{9,... | collective-permute-start | bytes 110600 | tf_op jit(solution)/shard_map/ppermute | solution.py:31
  15.2 0.3 %collective-permute-start.6 = (f32[48,128]{1,0:T(8,128)S(1)}, f32[48,128]{1,0:T(8,128)S(1)}, u32[]{:S(2)}, u32[]{:S(2)}) collective-permute-start(f32[48,128]{1,0:T(8,128)S(1)} %get-tuple-element.18), channel_id=1, source_target_pairs={{0,9},{1,8},{2,10},{3,11},{4,12},{5,13},{6,14},{7,15},{8,1},{9,0},... | collective-permute-start | bytes 73736 | tf_op jit(solution)/shard_map/ppermute | solution.py:31
  15.5 1.3 %collective-permute-done.5.far_ref = f32[24,384]{1,0:T(8,128)S(1)} collective-permute-done((f32[24,384]{1,0:T(8,128)S(1)}, f32[24,384]{1,0:T(8,128)S(1)}, u32[]{:S(2)}, u32[]{:S(2)}) %collective-permute-start.5) | collective-permute-done | bytes 36896 | tf_op jit(solution)/shard_map/ppermute | solution.py:31
  16.8 0.1 shard_map.41
  16.9 0.1 collective-permute-start.7
  17.0 0.1 shard_map.40.home_ref
  17.1 1.3 %collective-permute-done.6.near_ref = f32[48,128]{1,0:T(8,128)S(1)} collective-permute-done((f32[48,128]{1,0:T(8,128)S(1)}, f32[48,128]{1,0:T(8,128)S(1)}, u32[]{:S(2)}, u32[]{:S(2)}) %collective-permute-start.6) | collective-permute-done | bytes 24608 | tf_op jit(solution)/shard_map/ppermute | solution.py:31
  18.4 0.0 collective-permute-done.7.other_ref
  18.4 0.8 %shard_map.42 = f32[48,96]{1,0:T(8,128)} custom-call(f32[48,128]{1,0:T(8,128)S(1)} %shard_map.40.home_ref, f32[48,128]{1,0:T(8,128)S(1)} %collective-permute-done.6.near_ref, f32[48,128]{1,0:T(8,128)S(1)} %collective-permute-done.7.other_ref), custom_call_target="tpu_custom_call" | custom-call | tf_op jit(solution)/shard_map/pallas_call | solution.py:212
  (5 shorter events, 0.1 us)
Async XLA Ops:
  2.5 2.8 %collective-permute-start.2 = (f32[2,48,384]{2,1,0:T(8,128)S(1)}, f32[2,48,384]{2,1,0:T(8,128)S(1)}, u32[]{:S(2)}, u32[]{:S(2)}) collective-permute-start(f32[2,48,384]{2,1,0:T(8,128)S(1)} %get-tuple-element.13), channel_id=1, source_target_pairs={{0,1},{1,0},{2,3},{3,2},{4,5},{5,4},{6,7},{7,6},{8,9},{9,8},{10,11... | collective-permute-start | bytes 442376 | tf_op jit(solution)/shard_map/ppermute | solution.py:31
  2.7 6.8 %collective-permute-start = (f32[2,48,384]{2,1,0:T(8,128)S(1)}, f32[2,48,384]{2,1,0:T(8,128)S(1)}, u32[]{:S(2)}, u32[]{:S(2)}) collective-permute-start(f32[2,48,384]{2,1,0:T(8,128)S(1)} %get-tuple-element.15), channel_id=1, source_target_pairs={{0,4},{1,5},{2,6},{3,7},{4,0},{5,1},{6,2},{7,3},{8,13},{9,12},{10,... | collective-permute-start | bytes 442376 | tf_op jit(solution)/shard_map/ppermute | solution.py:31
  5.4 4.9 %collective-permute-start.3 = (f32[48,384]{1,0:T(8,128)S(1)}, f32[48,384]{1,0:T(8,128)S(1)}, u32[]{:S(2)}, u32[]{:S(2)}) collective-permute-start(f32[48,384]{1,0:T(8,128)S(1)} %get-tuple-element.9), channel_id=1, source_target_pairs={{0,3},{1,2},{2,1},{3,0},{4,7},{5,6},{6,5},{7,4},{8,10},{9,11},{10,... | collective-permute-start | bytes 221192 | tf_op jit(solution)/shard_map/ppermute | solution.py:31
  6.9 5.1 %collective-permute-start.4 = (f32[48,384]{1,0:T(8,128)S(1)}, f32[48,384]{1,0:T(8,128)S(1)}, u32[]{:S(2)}, u32[]{:S(2)}) collective-permute-start(f32[48,384]{1,0:T(8,128)S(1)} %get-tuple-element.10), channel_id=1, source_target_pairs={{0,7},{1,6},{2,5},{3,4},{4,3},{5,2},{6,1},{7,0},{8,14},{9,15},{10,... | collective-permute-start | bytes 221192 | tf_op jit(solution)/shard_map/ppermute | solution.py:31
  9.5 2.5 %collective-permute-start.1 = (f32[48,384]{1,0:T(8,128)S(1)}, f32[48,384]{1,0:T(8,128)S(1)}, u32[]{:S(2)}, u32[]{:S(2)}) collective-permute-start(f32[48,384]{1,0:T(8,128)S(1)} %get-tuple-element.16), channel_id=1, source_target_pairs={{0,1},{1,0},{2,3},{3,2},{4,5},{5,4},{6,7},{7,6},{8,9},{9,8},{10,11... | collective-permute-start | bytes 221192 | tf_op jit(solution)/shard_map/ppermute | solution.py:31
  12.1 4.7 %collective-permute-start.5 = (f32[24,384]{1,0:T(8,128)S(1)}, f32[24,384]{1,0:T(8,128)S(1)}, u32[]{:S(2)}, u32[]{:S(2)}) collective-permute-start(f32[24,384]{1,0:T(8,128)S(1)} %get-tuple-element.12), channel_id=1, source_target_pairs={{0,17},{1,25},{2,26},{3,18},{4,21},{5,29},{6,31},{7,23},{8,16},{9,... | collective-permute-start | bytes 110600 | tf_op jit(solution)/shard_map/ppermute | solution.py:31
  15.2 3.3 %collective-permute-start.6 = (f32[48,128]{1,0:T(8,128)S(1)}, f32[48,128]{1,0:T(8,128)S(1)}, u32[]{:S(2)}, u32[]{:S(2)}) collective-permute-start(f32[48,128]{1,0:T(8,128)S(1)} %get-tuple-element.18), channel_id=1, source_target_pairs={{0,9},{1,8},{2,10},{3,11},{4,12},{5,13},{6,14},{7,15},{8,1},{9,0},... | collective-permute-start | bytes 73736 | tf_op jit(solution)/shard_map/ppermute | solution.py:31
  16.9 1.5 %collective-permute-start.7 = (f32[48,128]{1,0:T(8,128)S(1)}, f32[48,128]{1,0:T(8,128)S(1)}, u32[]{:S(2)}, u32[]{:S(2)}) collective-permute-start(f32[48,128]{1,0:T(8,128)S(1)} %shard_map.41), channel_id=1, source_target_pairs={{0,1},{1,0},{2,3},{3,2},{4,5},{5,4},{6,7},{7,6},{8,9},{9,8},{10,11... | collective-permute-start | bytes 73736 | tf_op jit(solution)/shard_map/ppermute | solution.py:31

commit v10 on v9

--- a/solution.py
+++ b/solution.py
@@ -108,13 +108,12 @@
     x, y, z, core = place()
     for z_to in range(4):
         tile_ref[jnp.minimum(z ^ z_to, 2), :, :cols] = total[:, cols * z_to : cols * (z_to + 1)]
-    turned = pltpu.roll(total, nbasis // 2, 1)
     lane = lax.broadcasted_iota(jnp.int32, (half, nbasis), 1)
-    low = lane < nbasis // 2
     high_far = jnp.full_like(lane, z // 2) == 0
-    far_ref[...] = jnp.where(
-        high_far, jnp.where(low, turned[:half], total[half:]), jnp.where(low, total[:half], turned[half:])
-    )
+    moved = pltpu.roll(jnp.where(high_far, total[:half], total[half:]), nbasis // 2, 1)
+    kept = jnp.where(high_far, total[half:], total[:half])
+    low = (lane < nbasis // 2).astype(jnp.int32)
+    far_ref[...] = jnp.where(low == high_far.astype(jnp.int32), moved, kept)
 
 
 def part_of(far_ref, parity):

time: 19.4 us -> 19.4 us (level)
  no operation moved by 1% of the time
where the time goes in v10:
time: 19.4 us; the launch traced here: 19.2 us
  starting transfers between devices  9.51 us (49%)
  waiting for transfers between devices  5.92 us (31%)
  Pallas kernels  3.66 us (19%)
    ppermute x8, starting transfers between devices, swap(): return lax.ppermute(value, BOTH, pairs(moves))  9.51 us
    ppermute x8, waiting for transfers between devices, swap(): return lax.ppermute(value, BOTH, pairs(moves))  5.92 us
    pallas_call x1, Pallas kernels, fast_shards(): pl.pallas_call(product_kernel, out_shape=jax.ShapeDtypeStruct((8, rows, n...  2.48 us
    pallas_call x1, Pallas kernels, fast_shards(): pl.pallas_call(turn_kernel, out_shape=jax.ShapeDtypeStruct((rows, cols),...  0.77 us
  transfers between devices with their start and end apart: 8, of which 4 were waited for; matrix products, arithmetic and copies ran while one was open for 0% of the time, Pallas kernels for 2%

profile of v10, /device:TPU:1, one launch (start us, length us, event | category | flops | bytes accessed | tf_op | source)
XLA Modules:
  0.0 19.2 jit_solution(18061869665976194419)
XLA Ops:
  0.0 2.5 %shard_map.37 = f32[8,48,384]{2,1,0:T(8,128)S(1)} custom-call(s32[3,3]{1,0:T(4,128)} %pattern_hbm.1, bf16[1024,384]{1,0:T(8,128)(2,1)} %bitcast.10, bf16[1024,384]{1,0:T(8,128)(2,1)} %bitcast.11), custom_call_target="tpu_custom_call" | custom-call | tf_op jit(solution)/shard_map/pallas_call | solution.py:154
  2.5 0.1 collective-permute-start.2
  2.7 2.7 %collective-permute-start = (f32[2,48,384]{2,1,0:T(8,128)S(1)}, f32[2,48,384]{2,1,0:T(8,128)S(1)}, u32[]{:S(2)}, u32[]{:S(2)}) collective-permute-start(f32[2,48,384]{2,1,0:T(8,128)S(1)} %get-tuple-element.15), channel_id=1, source_target_pairs={{0,4},{1,5},{2,6},{3,7},{4,0},{5,1},{6,2},{7,3},{8,13},{9,12},{10,... | collective-permute-start | bytes 442376 | tf_op jit(solution)/shard_map/ppermute | solution.py:31
  5.4 0.0 collective-permute-done.2.came_ref
  5.4 1.5 %collective-permute-start.3 = (f32[48,384]{1,0:T(8,128)S(1)}, f32[48,384]{1,0:T(8,128)S(1)}, u32[]{:S(2)}, u32[]{:S(2)}) collective-permute-start(f32[48,384]{1,0:T(8,128)S(1)} %get-tuple-element.9), channel_id=1, source_target_pairs={{0,3},{1,2},{2,1},{3,0},{4,7},{5,6},{6,5},{7,4},{8,10},{9,11},{10,... | collective-permute-start | bytes 221192 | tf_op jit(solution)/shard_map/ppermute | solution.py:31
  6.9 1.0 %collective-permute-start.4 = (f32[48,384]{1,0:T(8,128)S(1)}, f32[48,384]{1,0:T(8,128)S(1)}, u32[]{:S(2)}, u32[]{:S(2)}) collective-permute-start(f32[48,384]{1,0:T(8,128)S(1)} %get-tuple-element.10), channel_id=1, source_target_pairs={{0,7},{1,6},{2,5},{3,4},{4,3},{5,2},{6,1},{7,0},{8,14},{9,15},{10,... | collective-permute-start | bytes 221192 | tf_op jit(solution)/shard_map/ppermute | solution.py:31
  7.9 1.6 %collective-permute-done = f32[2,48,384]{2,1,0:T(8,128)S(1)} collective-permute-done((f32[2,48,384]{2,1,0:T(8,128)S(1)}, f32[2,48,384]{2,1,0:T(8,128)S(1)}, u32[]{:S(2)}, u32[]{:S(2)}) %collective-permute-start) | collective-permute-done | bytes 147488 | tf_op jit(solution)/shard_map/ppermute | solution.py:31
  9.5 0.7 %collective-permute-start.1 = (f32[48,384]{1,0:T(8,128)S(1)}, f32[48,384]{1,0:T(8,128)S(1)}, u32[]{:S(2)}, u32[]{:S(2)}) collective-permute-start(f32[48,384]{1,0:T(8,128)S(1)} %get-tuple-element.16), channel_id=1, source_target_pairs={{0,1},{1,0},{2,3},{3,2},{4,5},{5,4},{6,7},{7,6},{8,9},{9,8},{10,11... | collective-permute-start | bytes 221192 | tf_op jit(solution)/shard_map/ppermute | solution.py:31
  10.2 0.0 collective-permute-done.3.b_ref
  10.2 1.7 %collective-permute-done.4.c_ref = f32[48,384]{1,0:T(8,128)S(1)} collective-permute-done((f32[48,384]{1,0:T(8,128)S(1)}, f32[48,384]{1,0:T(8,128)S(1)}, u32[]{:S(2)}, u32[]{:S(2)}) %collective-permute-start.4) | collective-permute-done | bytes 73760 | tf_op jit(solution)/shard_map/ppermute | solution.py:31
  12.0 0.0 collective-permute-done.1.a_ref
  12.0 0.1 shard_map.39
  12.1 3.1 %collective-permute-start.5 = (f32[24,384]{1,0:T(8,128)S(1)}, f32[24,384]{1,0:T(8,128)S(1)}, u32[]{:S(2)}, u32[]{:S(2)}) collective-permute-start(f32[24,384]{1,0:T(8,128)S(1)} %get-tuple-element.12), channel_id=1, source_target_pairs={{0,17},{1,25},{2,26},{3,18},{4,21},{5,29},{6,31},{7,23},{8,16},{9,... | collective-permute-start | bytes 110600 | tf_op jit(solution)/shard_map/ppermute | solution.py:31
  15.2 0.3 %collective-permute-start.6 = (f32[48,128]{1,0:T(8,128)S(1)}, f32[48,128]{1,0:T(8,128)S(1)}, u32[]{:S(2)}, u32[]{:S(2)}) collective-permute-start(f32[48,128]{1,0:T(8,128)S(1)} %get-tuple-element.18), channel_id=1, source_target_pairs={{0,9},{1,8},{2,10},{3,11},{4,12},{5,13},{6,14},{7,15},{8,1},{9,0},... | collective-permute-start | bytes 73736 | tf_op jit(solution)/shard_map/ppermute | solution.py:31
  15.5 1.3 %collective-permute-done.5.far_ref = f32[24,384]{1,0:T(8,128)S(1)} collective-permute-done((f32[24,384]{1,0:T(8,128)S(1)}, f32[24,384]{1,0:T(8,128)S(1)}, u32[]{:S(2)}, u32[]{:S(2)}) %collective-permute-start.5) | collective-permute-done | bytes 36896 | tf_op jit(solution)/shard_map/ppermute | solution.py:31
  16.8 0.1 shard_map.41
  16.9 0.1 collective-permute-start.7
  17.0 0.1 shard_map.40.home_ref
  17.1 1.3 %collective-permute-done.6.near_ref = f32[48,128]{1,0:T(8,128)S(1)} collective-permute-done((f32[48,128]{1,0:T(8,128)S(1)}, f32[48,128]{1,0:T(8,128)S(1)}, u32[]{:S(2)}, u32[]{:S(2)}) %collective-permute-start.6) | collective-permute-done | bytes 24608 | tf_op jit(solution)/shard_map/ppermute | solution.py:31
  18.4 0.0 collective-permute-done.7.other_ref
  18.4 0.8 %shard_map.42 = f32[48,96]{1,0:T(8,128)} custom-call(f32[48,128]{1,0:T(8,128)S(1)} %shard_map.40.home_ref, f32[48,128]{1,0:T(8,128)S(1)} %collective-permute-done.6.near_ref, f32[48,128]{1,0:T(8,128)S(1)} %collective-permute-done.7.other_ref), custom_call_target="tpu_custom_call" | custom-call | tf_op jit(solution)/shard_map/pallas_call | solution.py:211
  (5 shorter events, 0.1 us)
Async XLA Ops:
  2.5 2.8 %collective-permute-start.2 = (f32[2,48,384]{2,1,0:T(8,128)S(1)}, f32[2,48,384]{2,1,0:T(8,128)S(1)}, u32[]{:S(2)}, u32[]{:S(2)}) collective-permute-start(f32[2,48,384]{2,1,0:T(8,128)S(1)} %get-tuple-element.13), channel_id=1, source_target_pairs={{0,1},{1,0},{2,3},{3,2},{4,5},{5,4},{6,7},{7,6},{8,9},{9,8},{10,11... | collective-permute-start | bytes 442376 | tf_op jit(solution)/shard_map/ppermute | solution.py:31
  2.7 6.8 %collective-permute-start = (f32[2,48,384]{2,1,0:T(8,128)S(1)}, f32[2,48,384]{2,1,0:T(8,128)S(1)}, u32[]{:S(2)}, u32[]{:S(2)}) collective-permute-start(f32[2,48,384]{2,1,0:T(8,128)S(1)} %get-tuple-element.15), channel_id=1, source_target_pairs={{0,4},{1,5},{2,6},{3,7},{4,0},{5,1},{6,2},{7,3},{8,13},{9,12},{10,... | collective-permute-start | bytes 442376 | tf_op jit(solution)/shard_map/ppermute | solution.py:31
  5.4 4.9 %collective-permute-start.3 = (f32[48,384]{1,0:T(8,128)S(1)}, f32[48,384]{1,0:T(8,128)S(1)}, u32[]{:S(2)}, u32[]{:S(2)}) collective-permute-start(f32[48,384]{1,0:T(8,128)S(1)} %get-tuple-element.9), channel_id=1, source_target_pairs={{0,3},{1,2},{2,1},{3,0},{4,7},{5,6},{6,5},{7,4},{8,10},{9,11},{10,... | collective-permute-start | bytes 221192 | tf_op jit(solution)/shard_map/ppermute | solution.py:31
  6.9 5.1 %collective-permute-start.4 = (f32[48,384]{1,0:T(8,128)S(1)}, f32[48,384]{1,0:T(8,128)S(1)}, u32[]{:S(2)}, u32[]{:S(2)}) collective-permute-start(f32[48,384]{1,0:T(8,128)S(1)} %get-tuple-element.10), channel_id=1, source_target_pairs={{0,7},{1,6},{2,5},{3,4},{4,3},{5,2},{6,1},{7,0},{8,14},{9,15},{10,... | collective-permute-start | bytes 221192 | tf_op jit(solution)/shard_map/ppermute | solution.py:31
  9.5 2.5 %collective-permute-start.1 = (f32[48,384]{1,0:T(8,128)S(1)}, f32[48,384]{1,0:T(8,128)S(1)}, u32[]{:S(2)}, u32[]{:S(2)}) collective-permute-start(f32[48,384]{1,0:T(8,128)S(1)} %get-tuple-element.16), channel_id=1, source_target_pairs={{0,1},{1,0},{2,3},{3,2},{4,5},{5,4},{6,7},{7,6},{8,9},{9,8},{10,11... | collective-permute-start | bytes 221192 | tf_op jit(solution)/shard_map/ppermute | solution.py:31
  12.1 4.7 %collective-permute-start.5 = (f32[24,384]{1,0:T(8,128)S(1)}, f32[24,384]{1,0:T(8,128)S(1)}, u32[]{:S(2)}, u32[]{:S(2)}) collective-permute-start(f32[24,384]{1,0:T(8,128)S(1)} %get-tuple-element.12), channel_id=1, source_target_pairs={{0,17},{1,25},{2,26},{3,18},{4,21},{5,29},{6,31},{7,23},{8,16},{9,... | collective-permute-start | bytes 110600 | tf_op jit(solution)/shard_map/ppermute | solution.py:31
  15.2 3.3 %collective-permute-start.6 = (f32[48,128]{1,0:T(8,128)S(1)}, f32[48,128]{1,0:T(8,128)S(1)}, u32[]{:S(2)}, u32[]{:S(2)}) collective-permute-start(f32[48,128]{1,0:T(8,128)S(1)} %get-tuple-element.18), channel_id=1, source_target_pairs={{0,9},{1,8},{2,10},{3,11},{4,12},{5,13},{6,14},{7,15},{8,1},{9,0},... | collective-permute-start | bytes 73736 | tf_op jit(solution)/shard_map/ppermute | solution.py:31
  16.9 1.5 %collective-permute-start.7 = (f32[48,128]{1,0:T(8,128)S(1)}, f32[48,128]{1,0:T(8,128)S(1)}, u32[]{:S(2)}, u32[]{:S(2)}) collective-permute-start(f32[48,128]{1,0:T(8,128)S(1)} %shard_map.41), channel_id=1, source_target_pairs={{0,1},{1,0},{2,3},{3,2},{4,5},{5,4},{6,7},{7,6},{8,9},{9,8},{10,11... | collective-permute-start | bytes 73736 | tf_op jit(solution)/shard_map/ppermute | solution.py:31
